TPU v7x, 512 devices: a whole 4x8x8 slice. The times are simulated.
512 devices in a mesh: pool: 128 (over z, y, core), pb: 4 (over x).
Axes of the slice: x: 4, y: 8, z: 8, core: 2. Of those that a mesh axis runs over, the one named last changes fastest.
Arguments:
- adjoint_source: float32 [3, 4, 65536], P(None, None, 'pool'), may hold values from -6 to 6
- deviation: float32 [3, 4, 65536], P(None, None, 'pool'), may hold values from -6 to 6
- relax_time: float32 [4, 65536], P(None, 'pool'), may hold values from 0.3 to 3
- band_window: int32 [65536], P('pool'), may hold values from 1 to 15
- pair_src: int32 [524288], P(('pool', 'pb')), may hold values from 0 to 511
- pair_dst: int32 [524288], P(('pool', 'pb')), may hold values from 0 to 511
- bucket_fill: int32 [512, 128], P(('pool', 'pb')), may hold values from 2 to 8, as said below
- coupling: float32 [16, 524288], P(None, ('pool', 'pb')), may hold values from 0.05 to 0.5
Outputs:
- multiplier: float32 [3, 4, 65536], P(None, None, 'pool')
- coupling_grad: float32 [16, 524288], P(None, ('pool', 'pb'))
Inputs may be any that keep to these rules, and one draw needn't show every extreme that they name: The first bucket_fill[t, o] slots of the block of 8 slots that device t addresses to pool index o are live, the rest hold no pair. On every device at least one block is full.
All inputs are finite; a program needn't handle non-finite values.
Results may differ from a plain program's by a relative error of at most 0.00002.
Values sent between devices are 32-bit elements; how exact they have to be, the bound alone decides.
No kernel may reach another device: no remote copies, remote signals or barrier semaphores. Data moves between devices by JAX's collectives and lax.ppermute only.
A program may use at most 64 MiB of HBM per device.

v0:
```python
import jax
import jax.numpy as jnp
from jax import lax
from jax.sharding import PartitionSpec as P

ITERS = 2


def local(
    adjoint_source, deviation, relax_time, band_window, pair_src, pair_dst, bucket_fill, coupling
):
    dir_count, band_count, row_count = adjoint_source.shape
    slot_count = pair_src.shape[0]
    flat = dir_count * band_count
    capacity = slot_count // lax.axis_size("pool")
    slots = jnp.arange(slot_count, dtype=jnp.int32)
    filled = jnp.take(bucket_fill[0], slots // capacity)
    live = (slots % capacity < filled).astype(jnp.float32)
    bands = jnp.arange(band_count, dtype=jnp.int32)
    window = (band_window[None, :] >> bands[:, None] & 1).astype(jnp.float32)
    window_flat = jnp.broadcast_to(window[None], (dir_count, band_count, row_count)).reshape(
        flat, row_count
    )
    source = (window[None] * adjoint_source).reshape(flat, row_count)
    couple = coupling.reshape(band_count, band_count, slot_count)
    arrived = lax.all_to_all(pair_dst, "pool", split_axis=0, concat_axis=0, tiled=True)
    masked_dev = (window[None] * deviation).reshape(flat, row_count)
    returned_rows = jnp.take(masked_dev, arrived, axis=1)
    multiplier = source.reshape(dir_count, band_count, row_count)
    for step in range(ITERS):
        outgoing_moment = multiplier * relax_time[None]
        outgoing_picked = jnp.take(outgoing_moment, pair_src, axis=2)
        terms = couple[0][None] * outgoing_picked[:, 0][:, None]
        for band in range(1, band_count):
            terms = terms + couple[band][None] * outgoing_picked[:, band][:, None]
        received = lax.all_to_all(
            (terms * live).reshape(flat, slot_count),
            "pool",
            split_axis=1,
            concat_axis=1,
            tiled=True,
        )
        partial_rows = jnp.zeros((flat, row_count), jnp.float32).at[:, arrived].add(received)
        summed = lax.psum(partial_rows, "pb")
        whole = source + window_flat * summed
        multiplier = whole.reshape(dir_count, band_count, row_count)
    fetched = lax.all_to_all(returned_rows, "pool", split_axis=1, concat_axis=1, tiled=True)
    moment = multiplier * relax_time[None]
    picked = jnp.take(moment, pair_src, axis=2)
    farther = fetched.reshape(dir_count, band_count, slot_count)
    grads = picked[0][:, None] * farther[0][None]
    for direction in range(1, dir_count):
        grads = grads + picked[direction][:, None] * farther[direction][None]
    grads = grads * live
    return (multiplier, grads.reshape(band_count * band_count, slot_count))


def solution(mesh):
    in_specs = (
        P(None, None, "pool"),
        P(None, None, "pool"),
        P(None, "pool"),
        P("pool"),
        P(("pool", "pb")),
        P(("pool", "pb")),
        P(("pool", "pb"), None),
        P(None, ("pool", "pb")),
    )
    out_specs = (P(None, None, "pool"), P(None, ("pool", "pb")))
    return jax.shard_map(local, mesh=mesh, in_specs=in_specs, out_specs=out_specs, check_vma=False)
```

profile of v0, /device:TPU:1, one launch (start us, length us, event | category | flops | bytes accessed | tf_op | source)
XLA Modules:
  0.0 201.4 jit_solution(12874799055054429196)
XLA Ops:
  0.6 1.4 all_to_all.26
  2.0 18.4 %all-to-all-start = ((s32[128,8,1]{1,2,0:T(1,128)}), s32[128,8,1]{1,2,0:T(1,128)S(1)}, u32[]{:S(2)}, u32[]{:S(2)}) async-start(s32[128,8,1]{1,2,0:T(1,128)} %bitcast), calls=%async_computation | async-start | bytes 131072 | tf_op jit(solution)/shard_map/all_to_all | solution.py:26
  20.5 0.7 compare_and_fusion
  21.2 0.7 fusion.23
  21.9 0.7 and_convert_fusion
  22.6 6.6 %gather_fusion = s32[1024]{0:T(1024)S(1)} fusion(s32[128]{0:T(128)S(1)} %bitcast.48, s32[1024]{0:T(1024)S(1)} %broadcast_clamp_fusion), kind=kCustom, calls=%fused_computation.3 | custom fusion | bytes 12288 | tf_op jit(solution)/shard_map/jit(_take)/gather | solution.py:17
  29.6 0.4 copy.130
  30.0 3.6 %gather_fusion.2 = f32[1024,3,4]{2,1,0:T(4,128)S(1)} fusion(f32[3,4,512]{1,0,2:T(4,128)S(1)} %copy.130, s32[1024]{0:T(1024)S(1)} %fusion.23), kind=kCustom, calls=%fused_computation.clone | custom fusion | bytes 102400 | tf_op jit(solution)/shard_map/jit(_take)/gather | solution.py:32
  33.6 3.7 %select_bitcast_fusion.2 = f32[3,4,1024]{1,0,2:T(4,128)S(1)} fusion(f32[1024,3,4]{2,1,0:T(4,128)S(1)} %gather_fusion.2, pred[1024]{0:T(1024)(128)(4,1)S(1)} %compare_and_fusion), kind=kLoop, calls=%fused_computation.9 | loop fusion | flops 12288 | bytes 99328 | tf_op jit(solution)/shard_map/jit(_take)/select_n | solution.py:32
  37.3 5.9 %fusion.26 = (f32[3,1,1024]{1,0,2:T(4,128)}, f32[3,1,1024]{1,0,2:T(4,128)}, f32[3,1,1024]{1,0,2:T(4,128)}, f32[3,1,1024]{1,0,2:T(4,128)S(1)}) fusion(f32[3,4,1024]{1,0,2:T(4,128)S(1)} %select_bitcast_fusion.2), kind=kLoop, calls=%fused_computation.77 | loop fusion | bytes 98304 | tf_op jit(solution)/shard_map/slice | solution.py:33
  43.2 1.9 copy.131
  45.1 1.9 copy.134
  47.0 1.9 copy.133
  48.9 0.8 copy.132
  49.7 0.4 add.158
  50.5 1.6 copy.137
  52.1 13.7 %all-to-all-start.1 = ((f32[12,128,8]{0,2,1:T(8,128)}), f32[12,128,8]{0,2,1:T(8,128)S(1)}, u32[]{:S(2)}, u32[]{:S(2)}) async-start(f32[12,128,8]{0,2,1:T(8,128)} %copy.137), calls=%async_computation.1 | async-start | bytes 1048576 | tf_op jit(solution)/shard_map/all_to_all | solution.py:36
  65.9 0.5 broadcast.338
  66.4 0.8 reduce.3
  67.5 2.8 %gather_fusion.1 = f32[1024,12]{1,0:T(8,128)S(1)} fusion(f32[12,512]{0,1:T(8,128)S(1)} %copy.154, s32[1024]{0:T(1024)S(1)} %broadcast_clamp_fusion.1), kind=kCustom, calls=%fused_computation.4 | custom fusion | bytes 102400 | tf_op jit(solution)/shard_map/jit(_take)/gather | solution.py:28
  70.3 1.0 bitcast_select_fusion
  71.3 15.1 %all-to-all-done.1 = f32[12,128,8]{0,2,1:T(8,128)S(1)} async-done(((f32[12,128,8]{0,2,1:T(8,128)}), f32[12,128,8]{0,2,1:T(8,128)S(1)}, u32[]{:S(2)}, u32[]{:S(2)}) %all-to-all-start.1) | async-done | bytes 49184 | tf_op jit(solution)/shard_map/all_to_all | solution.py:36
  86.4 5.5 %all-to-all-start.3 = ((f32[12,128,8]{0,2,1:T(8,128)}), f32[12,128,8]{0,2,1:T(8,128)S(1)}, u32[]{:S(2)}, u32[]{:S(2)}) async-start(f32[12,128,8]{0,2,1:T(8,128)} %bitcast_select_fusion), calls=%async_computation.3 | async-start | bytes 1048576 | tf_op jit(solution)/shard_map/all_to_all | solution.py:47
  91.9 6.1 %scatter_custom_fusion = f32[12,512]{0,1:T(8,128)S(1)} fusion(s32[1024]{0:T(1024)S(1)} %bitcast.61, f32[12,128,8]{0,2,1:T(8,128)S(1)} %all-to-all-done.1, f32[]{:T(128)} %constant.70.clone.1), kind=kCustom, calls=%fused_computation.16 | custom fusion | flops 12288 | bytes 548868 | tf_op jit(solution)/shard_map/scatter-add | solution.py:43
  98.2 14.2 %psum.14 = f32[12,512]{1,0:T(8,128)S(1)} all-reduce(f32[12,512]{1,0:T(8,128)S(1)} %copy.140), channel_id=1, replica_groups=mesh['pool'=128,'pb'=4] {'pb'}, use_global_device_ids=true, to_apply=%region_1.3 | all-reduce | flops 6144 | bytes 49152 | tf_op jit(solution)/shard_map/psum | solution.py:44
  112.4 1.3 copy.141
  113.8 4.8 %gather_fusion.3 = f32[1024,3,4]{2,1,0:T(4,128)S(1)} fusion(f32[3,4,512]{1,0,2:T(4,128)} %copy.141, s32[1024]{0:T(1024)S(1)} %fusion.23), kind=kCustom, calls=%fused_computation.1.clone | custom fusion | bytes 102400 | tf_op jit(solution)/shard_map/jit(_take)/gather | solution.py:32
  118.5 3.7 %select_bitcast_fusion.1 = f32[3,4,1024]{1,0,2:T(4,128)S(1)} fusion(f32[1024,3,4]{2,1,0:T(4,128)S(1)} %gather_fusion.3, pred[1024]{0:T(1024)(128)(4,1)S(1)} %compare_and_fusion), kind=kLoop, calls=%fused_computation.8 | loop fusion | flops 12288 | bytes 99328 | tf_op jit(solution)/shard_map/jit(_take)/select_n | solution.py:32
  122.3 5.9 %fusion.25 = (f32[3,1,1024]{1,0,2:T(4,128)}, f32[3,1,1024]{1,0,2:T(4,128)}, f32[3,1,1024]{1,0,2:T(4,128)}, f32[3,1,1024]{1,0,2:T(4,128)S(1)}) fusion(f32[3,4,1024]{1,0,2:T(4,128)S(1)} %select_bitcast_fusion.1), kind=kLoop, calls=%fused_computation.76 | loop fusion | bytes 98304 | tf_op jit(solution)/shard_map/slice | solution.py:33
  128.2 1.9 copy.142
  130.0 1.9 copy.145
  132.0 1.9 copy.144
  133.9 0.8 copy.143
  134.7 0.4 add.168
  135.2 1.6 copy.146
  136.9 16.5 %all-to-all-start.2 = ((f32[12,128,8]{0,2,1:T(8,128)}), f32[12,128,8]{0,2,1:T(8,128)S(1)}, u32[]{:S(2)}, u32[]{:S(2)}) async-start(f32[12,128,8]{0,2,1:T(8,128)} %copy.146), calls=%async_computation.2 | async-start | bytes 1048576 | tf_op jit(solution)/shard_map/all_to_all | solution.py:36
  153.4 0.3 slice_bitcast_fusion.2
  153.9 0.2 copy.159
  154.3 19.7 %all-to-all-done.2 = f32[12,128,8]{0,2,1:T(8,128)S(1)} async-done(((f32[12,128,8]{0,2,1:T(8,128)}), f32[12,128,8]{0,2,1:T(8,128)S(1)}, u32[]{:S(2)}, u32[]{:S(2)}) %all-to-all-start.2) | async-done | bytes 49184 | tf_op jit(solution)/shard_map/all_to_all | solution.py:36
  174.0 6.1 %scatter_custom_fusion.1 = f32[12,512]{0,1:T(8,128)S(1)} fusion(s32[1024]{0:T(1024)S(1)} %bitcast.62, f32[12,128,8]{0,2,1:T(8,128)S(1)} %all-to-all-done.2, f32[]{:T(128)} %constant.70.clone.1), kind=kCustom, calls=%fused_computation.14 | custom fusion | flops 12288 | bytes 548868 | tf_op jit(solution)/shard_map/scatter-add | solution.py:43
  180.2 11.0 %psum.15 = f32[12,512]{1,0:T(8,128)S(1)} all-reduce(f32[12,512]{1,0:T(8,128)S(1)} %copy.149), channel_id=1, replica_groups=mesh['pool'=128,'pb'=4] {'pb'}, use_global_device_ids=true, to_apply=%region_3.5 | all-reduce | flops 6144 | bytes 49152 | tf_op jit(solution)/shard_map/psum | solution.py:44
  191.3 0.4 copy.150
  191.7 3.6 %gather_fusion.4 = f32[1024,3,4]{2,1,0:T(4,128)S(1)} fusion(f32[3,4,512]{1,0,2:T(4,128)S(1)} %copy.150, s32[1024]{0:T(1024)S(1)} %fusion.23), kind=kCustom, calls=%fused_computation.2.clone | custom fusion | bytes 102400 | tf_op jit(solution)/shard_map/jit(_take)/gather | solution.py:49
  195.3 3.7 %select_bitcast_fusion = f32[3,4,1024]{1,0,2:T(4,128)S(1)} fusion(f32[1024,3,4]{2,1,0:T(4,128)S(1)} %gather_fusion.4, pred[1024]{0:T(1024)(128)(4,1)S(1)} %compare_and_fusion), kind=kLoop, calls=%fused_computation.7 | loop fusion | flops 12288 | bytes 99328 | tf_op jit(solution)/shard_map/jit(_take)/select_n | solution.py:49
  199.0 1.1 fusion.24
  200.3 0.2 copy.158
  200.5 0.2 copy.156
  200.8 0.6 broadcast_multiply_fusion.2
  (51 shorter events, 2.0 us)
Async XLA Ops:
  0.6 22.0 %copy-start = (s32[1,128]{1,0:T(1,128)S(1)}, s32[1,128]{1,0:T(1,128)}, u32[]{:S(2)}) copy-start(s32[1,128]{1,0:T(1,128)} %param.16) | copy-start | bytes 1540
  2.0 50.1 %all-to-all-start = ((s32[128,8,1]{1,2,0:T(1,128)}), s32[128,8,1]{1,2,0:T(1,128)S(1)}, u32[]{:S(2)}, u32[]{:S(2)}) async-start(s32[128,8,1]{1,2,0:T(1,128)} %bitcast), calls=%async_computation | async-start | bytes 131072 | tf_op jit(solution)/shard_map/all_to_all | solution.py:26
  22.6 6.9 %copy-start.3 = (f32[16,1024]{1,0:T(8,128)S(1)}, f32[16,1024]{1,0:T(8,128)}, u32[]{:S(2)}) copy-start(f32[16,1024]{1,0:T(8,128)} %param.17) | copy-start | bytes 196612
  22.6 6.9 %copy-start.2 = (f32[4,512]{1,0:T(4,128)S(1)}, f32[4,512]{1,0:T(4,128)}, u32[]{:S(2)}) copy-start(f32[4,512]{1,0:T(4,128)} %param.12) | copy-start | bytes 24580
  22.6 6.9 %copy-start.4 = (f32[3,4,512]{2,1,0:T(4,128)S(1)}, f32[3,4,512]{2,1,0:T(4,128)}, u32[]{:S(2)}) copy-start(f32[3,4,512]{2,1,0:T(4,128)} %param.10) | copy-start | bytes 73732
  22.6 6.9 %copy-start.5 = (f32[3,4,512]{2,1,0:T(4,128)S(1)}, f32[3,4,512]{2,1,0:T(4,128)}, u32[]{:S(2)}) copy-start(f32[3,4,512]{2,1,0:T(4,128)} %param.11) | copy-start | bytes 73732
  52.1 34.3 %all-to-all-start.1 = ((f32[12,128,8]{0,2,1:T(8,128)}), f32[12,128,8]{0,2,1:T(8,128)S(1)}, u32[]{:S(2)}, u32[]{:S(2)}) async-start(f32[12,128,8]{0,2,1:T(8,128)} %copy.137), calls=%async_computation.1 | async-start | bytes 1048576 | tf_op jit(solution)/shard_map/all_to_all | solution.py:36
  86.4 50.4 %all-to-all-start.3 = ((f32[12,128,8]{0,2,1:T(8,128)}), f32[12,128,8]{0,2,1:T(8,128)S(1)}, u32[]{:S(2)}, u32[]{:S(2)}) async-start(f32[12,128,8]{0,2,1:T(8,128)} %bitcast_select_fusion), calls=%async_computation.3 | async-start | bytes 1048576 | tf_op jit(solution)/shard_map/all_to_all | solution.py:47
  136.9 37.1 %all-to-all-start.2 = ((f32[12,128,8]{0,2,1:T(8,128)}), f32[12,128,8]{0,2,1:T(8,128)S(1)}, u32[]{:S(2)}, u32[]{:S(2)}) async-start(f32[12,128,8]{0,2,1:T(8,128)} %copy.146), calls=%async_computation.2 | async-start | bytes 1048576 | tf_op jit(solution)/shard_map/all_to_all | solution.py:36
  191.3 7.8 %copy-start.1 = (f32[3,4,512]{2,1,0:T(4,128)}, f32[3,4,512]{2,1,0:T(4,128)S(1)}, u32[]{:S(2)}) copy-start(f32[3,4,512]{2,1,0:T(4,128)S(1)} %reshape.278) | copy-start | bytes 73732
where the time goes:
time: 204 us; the launch traced here: 201 us
  local copies, waits for them, and re-layouts  57.9 us (28%)
  starting transfers between devices  54.2 us (27%)
  waiting for transfers between devices  34.8 us (17%)
  other arithmetic  28.4 us (14%)
  blocking collectives  25.2 us (12%)
    all_to_all x2, waiting for transfers between devices, local(): lax.all_to_all((terms * live).reshape(flat, slot_count), 'pool', split_ax...  34.7 us
    all_to_all x2, starting transfers between devices, local(): lax.all_to_all((terms * live).reshape(flat, slot_count), 'pool', split_ax...  30.2 us
    psum x2, blocking collectives, local(): summed = lax.psum(partial_rows, 'pb')  25.2 us
    all_to_all x1, starting transfers between devices, local(): lax.all_to_all(pair_dst, 'pool', split_axis=0, concat_axis=0, tiled=True)  18.4 us
    slice x5, local copies, waits for them, and re-layouts, local(): terms = couple[0][None] * outgoing_picked[:, 0][:, None]  15.5 us
    scatter-add x2, other arithmetic, local(): jnp.zeros((flat, row_count), jnp.float32).at[:, arrived].add(received)  12.2 us
    slice x6, local copies, waits for them, and re-layouts, local(): terms = terms + couple[band][None] * outgoing_picked[:, band][:, None]  9.26 us
    gather x2, local copies, waits for them, and re-layouts, local(): outgoing_picked = jnp.take(outgoing_moment, pair_src, axis=2)  8.32 us
  transfers between devices with their start and end apart: 4, of which 2 were waited for; matrix products, arithmetic and copies ran while one was open for 34% of the time, Pallas kernels for 0%

commit v1 on v0

v1 whole, which is shorter than its diff:
```python
import functools

import jax
import jax.numpy as jnp
from jax import lax
from jax.experimental import pallas as pl
from jax.experimental.pallas import tpu as pltpu
from jax.sharding import PartitionSpec as P

ITERS = 2
WIDTH = 16
F32 = jnp.float32
BF16 = jnp.bfloat16
MIB = 1024 * 1024


def split3(x):
    high = x.astype(BF16)
    rest = x - high.astype(F32)
    middle = rest.astype(BF16)
    low = (rest - middle.astype(F32)).astype(BF16)
    return jnp.concatenate([high, middle, low], axis=0)


def tiles_of(x):
    parts = split3(x)
    width = min(128, x.shape[1])
    return jnp.concatenate([parts[:, t : t + width] for t in range(0, x.shape[1], width)], axis=0)


def whole(parts):
    return parts[:16] + parts[16:32] + parts[32:48]


def select(x, index):
    width = min(128, x.shape[1])
    rows = lax.broadcasted_iota(jnp.int32, (width, index.shape[1]), 0)
    hot = jnp.where(rows == (index & (width - 1)), 1.0, 0.0).astype(BF16)
    found = jnp.dot(tiles_of(x), hot, preferred_element_type=F32)
    at = jnp.broadcast_to(index, (16, index.shape[1])) >> (width.bit_length() - 1)
    total = whole(found[:48])
    for tile in range(1, x.shape[1] // width):
        total = jnp.where(at == tile, whole(found[48 * tile : 48 * tile + 48]), total)
    return total


def pick(x, index):
    parts = []
    width = min(128, index.shape[1])
    for first in range(0, index.shape[1], width):
        at = jnp.broadcast_to(index[:, first : first + width], (x.shape[0], width))
        part = jnp.zeros(at.shape, F32)
        for tile in range(x.shape[1] // 128):
            columns = x[:, 128 * tile : 128 * (tile + 1)]
            found = jnp.take_along_axis(columns, at & 127, axis=1, mode="promise_in_bounds")
            part = jnp.where(at >> 7 == tile, found, part)
        parts.append(part)
    return jnp.concatenate(parts, axis=1)


def rows16(ref):
    return jnp.concatenate([ref[0], ref[1], ref[2], jnp.zeros_like(ref[0])], axis=0)


def window16(window_ref):
    rows = lax.broadcasted_iota(jnp.int32, (16, window_ref.shape[1]), 0)
    return ((window_ref[...] >> (rows & 3)) & 1).astype(F32)


def live_row(fill_ref, slots):
    owners = fill_ref.shape[1]
    capacity = slots // owners
    fill = jnp.broadcast_to(fill_ref[...].astype(F32), (8, owners))
    lane = lax.broadcasted_iota(jnp.int32, (8, owners), 1)
    place = (lane & (capacity - 1)).astype(F32)
    parts = []
    for first in range(0, owners, owners // capacity):
        filled = jnp.take_along_axis(fill, first + (lane >> (capacity.bit_length() - 1)), axis=1, mode="promise_in_bounds")
        parts.append(jnp.where(place < filled, 1.0, 0.0)[:1])
    return jnp.concatenate(parts, axis=1)


def repeat_rows(x, first, step, count):
    row = lax.broadcasted_iota(jnp.int32, (16, x.shape[1]), 0)
    out = jnp.broadcast_to(x[first : first + 1], row.shape)
    for i in range(1, count):
        out = jnp.where(row >= 4 * i, x[first + step * i : first + step * i + 1], out)
    return out


def scatter_terms(picked, live, couple):
    total = None
    for band in range(4):
        block = couple[4 * band : 4 * band + 4]
        block = jnp.concatenate([block, block, block, jnp.zeros_like(block)], axis=0)
        term = block * repeat_rows(picked, band, 4, 3)
        total = term if total is None else total + term
    return total * live


def slots_to_rows(x, flat_ref):
    owners = x.shape[1] // 8
    flat_ref[...] = x.T
    return jnp.concatenate([flat_ref[pl.ds(j, owners, stride=8), :] for j in range(8)], axis=1)


def pack(x):
    half = x.shape[1] // 2
    tail = jnp.concatenate([x[8:12, :half], x[8:12, half:]], axis=0)
    return jnp.concatenate([x[:8], tail], axis=1)


def unpack(x):
    whole = x.shape[1] * 2 // 3
    tail = jnp.concatenate([x[:4, whole:], x[4:, whole:]], axis=1)
    return jnp.concatenate([x[:8, :whole], jnp.concatenate([tail, jnp.zeros_like(tail)], axis=0)], axis=0)


def received_slots(rows):
    turned = rows.T
    return jnp.concatenate([turned[WIDTH * j : WIDTH * (j + 1)] for j in range(8)], axis=1)


def sums_of(slots, rows, states):
    turned = rows.T.astype(jnp.int32)
    index = jnp.concatenate([turned[WIDTH * j + 12 : WIDTH * j + 13] for j in range(8)], axis=1)
    state = lax.broadcasted_iota(jnp.int32, (states, index.shape[1]), 0)
    hot = jnp.where(state == index, 1.0, 0.0).astype(BF16)
    both = (((1,), (1,)), ((), ()))
    return whole(lax.dot_general(split3(slots), hot, both, preferred_element_type=F32))


def zero_kernel(out_ref):
    out_ref[...] = jnp.zeros_like(out_ref)


def first_kernel(
    zero_ref, couple_ref, source_ref, relax_ref, window_ref, src_ref, dst_ref, fill_ref, out_ref, flat_ref
):
    live = live_row(fill_ref, src_ref.shape[1])
    relax = jnp.concatenate([relax_ref[...]] * 4, axis=0)
    moment = rows16(source_ref) * window16(window_ref) * relax
    terms = scatter_terms(pick(moment, src_ref[...]), live, couple_ref[...])
    row = lax.broadcasted_iota(jnp.int32, terms.shape, 0)
    terms = jnp.where(row == 12, dst_ref[...].astype(F32) + zero_ref[:1, :1], terms)
    out_ref[...] = slots_to_rows(terms, flat_ref)


def gather_kernel(rows_ref, index_ref, out_ref, *, states):
    senders = index_ref.shape[0]
    depth = rows_ref.shape[0] // senders
    rows = rows_ref[...] if depth == 1 else rows_ref[pl.ds(0, senders, stride=depth), :]
    packed = pack(sums_of(received_slots(rows), index_ref[...], states))
    for i in range(out_ref.shape[0]):
        out_ref[i] = packed


def returned_rows(dev_ref, window_ref, index_ref):
    masked = rows16(dev_ref) * window16(window_ref)
    turned = index_ref[...].T.astype(jnp.int32)
    found = [pick(masked, turned[WIDTH * j + 12 : WIDTH * j + 13]) for j in range(8)]
    return jnp.concatenate(found, axis=0).T


def multiplier_of(part, source_ref, window_ref):
    window = window16(window_ref)
    return window * (rows16(source_ref) + unpack((part[0] + part[1]) + (part[2] + part[3])))


def second_kernel(
    parts_ref, index_ref, dev_ref, source_ref, relax_ref, window_ref, src_ref, fill_ref, couple_ref, out_ref, flat_ref
):
    senders = index_ref.shape[0]
    out_ref[pl.ds(1, senders, stride=2), :] = returned_rows(dev_ref, window_ref, index_ref)
    relax = jnp.concatenate([relax_ref[...]] * 4, axis=0)
    moment = relax * multiplier_of(parts_ref, source_ref, window_ref)
    live = live_row(fill_ref, src_ref.shape[1])
    terms = scatter_terms(select(moment, src_ref[...]), live, couple_ref[...])
    out_ref[pl.ds(0, senders, stride=2), :] = slots_to_rows(terms, flat_ref)


def last_kernel(
    parts_ref, rows_ref, source_ref, relax_ref, window_ref, src_ref, fill_ref, multiplier_ref, grad_ref, flat_ref
):
    owners = rows_ref.shape[0] // 2
    rows = rows_ref[pl.ds(1, owners, stride=2), :]
    for j in range(8):
        flat_ref[pl.ds(j, owners, stride=8), :] = rows[:, WIDTH * j : WIDTH * (j + 1)]
    fetched = flat_ref[...].T
    relax = jnp.concatenate([relax_ref[...]] * 4, axis=0)
    multiplier = multiplier_of(parts_ref, source_ref, window_ref)
    for d in range(3):
        multiplier_ref[d] = multiplier[4 * d : 4 * d + 4]
    picked = select(relax * multiplier, src_ref[...])
    total = None
    for d in range(3):
        far = fetched[4 * d : 4 * d + 4]
        term = repeat_rows(picked, 4 * d, 1, 4) * jnp.concatenate([far] * 4, axis=0)
        total = term if total is None else total + term
    grad_ref[...] = total * live_row(fill_ref, src_ref.shape[1])


def call(kernel, out_shape, scratch, *operands, cost=None):
    return pl.pallas_call(
        kernel,
        out_shape=out_shape,
        in_specs=[pl.BlockSpec(memory_space=pltpu.VMEM)] * len(operands),
        scratch_shapes=scratch,
        compiler_params=pltpu.CompilerParams(vmem_limit_bytes=24 * MIB),
        cost_estimate=cost,
    )(*operands)


def exchange(rows):
    pools = lax.axis_size("pool")
    x = rows.reshape(pools, -1, 128)
    return lax.all_to_all(x, "pool", 0, 0, tiled=True).reshape(rows.shape)


def share(part):
    return lax.all_to_all(part, "pb", 0, 0, tiled=True)


def local(
    adjoint_source, deviation, relax_time, band_window, pair_src, pair_dst, bucket_fill, coupling
):
    states = band_window.shape[0]
    slots = pair_src.shape[0]
    pools = lax.axis_size("pool")
    window = band_window.reshape(1, states)
    src = pair_src.reshape(1, slots)
    dst = pair_dst.reshape(1, slots)
    sds = jax.ShapeDtypeStruct
    flat = pltpu.VMEM((slots, WIDTH), F32)
    partial = sds((lax.axis_size("pb"), 8, states * 3 // 2), F32)

    cost = pl.CostEstimate(flops=10**10, bytes_accessed=0, transcendentals=0)
    zero = call(zero_kernel, sds((8, 128), F32), [], cost=cost)
    sent = call(
        first_kernel, sds((pools, 128), F32), [flat],
        zero, coupling, adjoint_source, relax_time, window, src, dst, bucket_fill,
    )
    index = exchange(sent)
    gather = functools.partial(gather_kernel, states=states)
    parts = share(call(gather, partial, [], index, index))
    sent = call(
        second_kernel, sds((2 * pools, 128), F32), [flat],
        parts, index, deviation, adjoint_source, relax_time, window, src, bucket_fill, coupling,
    )
    rows = exchange(sent)
    parts = share(call(gather, partial, [], rows, index))
    return call(
        last_kernel, (sds(adjoint_source.shape, F32), sds(coupling.shape, F32)), [flat],
        parts, rows, adjoint_source, relax_time, window, src, bucket_fill,
    )


def solution(mesh):
    in_specs = (
        P(None, None, "pool"),
        P(None, None, "pool"),
        P(None, "pool"),
        P("pool"),
        P(("pool", "pb")),
        P(("pool", "pb")),
        P(("pool", "pb"), None),
        P(None, ("pool", "pb")),
    )
    out_specs = (P(None, None, "pool"), P(None, ("pool", "pb")))
    return jax.shard_map(local, mesh=mesh, in_specs=in_specs, out_specs=out_specs, check_vma=False)
```

time: 204 us -> 69.8 us (0.34); the launches traced: 201 us -> 69.5 us
  local copies, waits for them, and re-layouts: 57.9 us -> 0.81 us
  starting transfers between devices: 54.2 us -> 0 us
  blocking collectives: 25.2 us -> 64.7 us
  waiting for transfers between devices: 34.8 us -> 0 us
  other arithmetic: 28.4 us -> 0 us
  Pallas kernels: 0 us -> 3.27 us
    all_to_all x0 -> x4, blocking collectives: none -> 64.7 us  [the longest x2 49 us: exchange(): return lax.all_to_all(x, 'pool', 0, 0, tiled=True).reshape(rows.shape)]
    all_to_all x4 -> x0, starting transfers between devices: 54.2 us -> none  [the longest x2 30.2 us: local(): lax.all_to_all((terms * live).reshape(flat, slot_count), 'pool', split_ax...]
    all_to_all x4 -> x0, waiting for transfers between devices: 34.8 us -> none  [the longest x2 34.7 us: local(): lax.all_to_all((terms * live).reshape(flat, slot_count), 'pool', split_ax...]
    slice x12 -> x0, local copies, waits for them, and re-layouts: 25.9 us -> none  [the longest x5 15.5 us: local(): terms = couple[0][None] * outgoing_picked[:, 0][:, None]]
    psum x2 -> x0, blocking collectives: 25.2 us -> none  [local(): summed = lax.psum(partial_rows, 'pb')]
    gather x7 -> x0, local copies, waits for them, and re-layouts: 21.4 us -> none  [the longest x2 8.32 us: local(): outgoing_picked = jnp.take(outgoing_moment, pair_src, axis=2)]
    scatter-add x2 -> x0, other arithmetic: 12.2 us -> none  [local(): jnp.zeros((flat, row_count), jnp.float32).at[:, arrived].add(received)]
    select_n x6 -> x0, other arithmetic: 12.2 us -> none  [the longest x2 7.48 us: local(): outgoing_picked = jnp.take(outgoing_moment, pair_src, axis=2)]
  transfers between devices with their start and end apart: 4 -> 0, of which waited for: 2 -> 0; matrix products, arithmetic and copies ran while one was open for 34% -> 0% of each run, Pallas kernels for 0% -> 0%
where the time goes in v1:
time: 69.8 us; the launch traced here: 69.5 us
  blocking collectives  64.7 us (93%)
  Pallas kernels  3.27 us (5%)
  local copies, waits for them, and re-layouts  0.81 us (1%)
  between operations  0.72 us (1%)
    all_to_all x2, blocking collectives, exchange(): return lax.all_to_all(x, 'pool', 0, 0, tiled=True).reshape(rows.shape)  49 us
    all_to_all x2, blocking collectives, share(): return lax.all_to_all(part, 'pb', 0, 0, tiled=True)  15.7 us
    pallas_call x6, Pallas kernels, call(): pl.pallas_call(kernel, out_shape=out_shape, in_specs=[pl.BlockSpec(memory...  3.27 us

profile of v1, /device:TPU:1, one launch (start us, length us, event | category | flops | bytes accessed | tf_op | source)
XLA Modules:
  0.0 69.5 jit_solution(13417470247421219)
XLA Ops:
  0.6 0.0 copy-start.1
  0.6 0.0 copy-start
  0.7 0.0 copy-start.2
  0.7 0.0 copy-start.5
  0.7 0.0 copy-start.7
  0.7 0.0 copy-start.3
  0.7 0.0 copy-start.6
  0.7 0.7 copy-done.1
  1.4 0.1 copy-done
  1.5 0.0 copy-done.2
  1.5 0.0 copy-done.5
  1.5 0.0 copy-done.7
  1.5 0.0 copy-done.3
  1.5 0.0 copy-done.6
  1.5 0.6 shard_map.96
  2.1 29.7 %all_to_all.20 = f32[128,1,128]{2,1,0:T(1,128)S(1)} all-to-all(f32[128,1,128]{2,1,0:T(1,128)S(1)} %bitcast.16), channel_id=1, replica_groups=mesh['pool'=128,'pb'=4] {'pool'}, dimensions={0} | all-to-all | bytes 131072 | tf_op jit(solution)/shard_map/all_to_all | solution.py:217
  31.8 0.5 shard_map.97
  32.2 0.0 copy-start.4
  32.2 8.6 %all_to_all.21.parts_ref = f32[4,8,768]{2,1,0:T(8,128)S(1)} all-to-all(f32[4,8,768]{2,1,0:T(8,128)S(1)} %shard_map.97), channel_id=1, replica_groups=mesh['pool'=128,'pb'=4] {'pb'}, dimensions={0} | all-to-all | bytes 196608 | tf_op jit(solution)/shard_map/all_to_all | solution.py:221
  40.9 0.0 copy-done.4
  40.9 0.6 shard_map.98
  41.5 19.4 %all_to_all.22 = f32[128,2,128]{2,1,0:T(2,128)S(1)} all-to-all(f32[128,2,128]{2,1,0:T(2,128)S(1)} %bitcast.15), channel_id=1, replica_groups=mesh['pool'=128,'pb'=4] {'pool'}, dimensions={0} | all-to-all | bytes 262144 | tf_op jit(solution)/shard_map/all_to_all | solution.py:217
  60.9 0.5 shard_map.99
  61.4 7.0 %all_to_all.23.parts_ref = f32[4,8,768]{2,1,0:T(8,128)S(1)} all-to-all(f32[4,8,768]{2,1,0:T(8,128)S(1)} %shard_map.99), channel_id=1, replica_groups=mesh['pool'=128,'pb'=4] {'pb'}, dimensions={0} | all-to-all | bytes 196608 | tf_op jit(solution)/shard_map/all_to_all | solution.py:221
  68.4 1.1 %shard_map.100 = (f32[3,4,512]{2,1,0:T(4,128)}, f32[16,1024]{1,0:T(8,128)}) custom-call(f32[4,8,768]{2,1,0:T(8,128)S(1)} %all_to_all.23.parts_ref, f32[256,128]{1,0:T(8,128)S(1)} %bitcast.14, f32[3,4,512]{2,1,0:T(4,128)S(1)} %copy-done.1, f32[4,512]{1,0:T(4,128)S(1)} %copy-done.2, s32[1,512]{1,0:T(1,128)S(1)} %bitcast.22, s32[1,1024]{1,0:T(1,128)S(1)} %bitcast.19, ...), custom_call_target="tpu_custom_call" | custom-call | tf_op jit(solution)/shard_map/pallas_call | solution.py:204
  (1 shorter events, 0.0 us)
Async XLA Ops:
  0.6 0.7 %copy-start.1 = (f32[3,4,512]{2,1,0:T(4,128)S(1)}, f32[3,4,512]{2,1,0:T(4,128)}, u32[]{:S(2)}) copy-start(f32[3,4,512]{2,1,0:T(4,128)} %source_ref.5) | copy-start | bytes 73732
  0.6 0.8 %copy-start = (f32[16,1024]{1,0:T(8,128)S(1)}, f32[16,1024]{1,0:T(8,128)}, u32[]{:S(2)}) copy-start(f32[16,1024]{1,0:T(8,128)} %couple_ref.3) | copy-start | bytes 196612
  0.7 0.8 %copy-start.2 = (f32[4,512]{1,0:T(4,128)S(1)}, f32[4,512]{1,0:T(4,128)}, u32[]{:S(2)}) copy-start(f32[4,512]{1,0:T(4,128)} %relax_ref.5) | copy-start | bytes 24580
  0.7 0.8 %copy-start.5 = (s32[512]{0:T(512)S(1)}, s32[512]{0:T(512)}, u32[]{:S(2)}) copy-start(s32[512]{0:T(512)} %param.11) | copy-start | bytes 6148
  0.7 0.8 %copy-start.7 = (s32[1024]{0:T(1024)S(1)}, s32[1024]{0:T(1024)}, u32[]{:S(2)}) copy-start(s32[1024]{0:T(1024)} %param.13) | copy-start | bytes 12292
  0.7 0.8 %copy-start.3 = (s32[1024]{0:T(1024)S(1)}, s32[1024]{0:T(1024)}, u32[]{:S(2)}) copy-start(s32[1024]{0:T(1024)} %param.12) | copy-start | bytes 12292
  0.7 0.8 %copy-start.6 = (s32[1,128]{1,0:T(1,128)S(1)}, s32[1,128]{1,0:T(1,128)}, u32[]{:S(2)}) copy-start(s32[1,128]{1,0:T(1,128)} %fill_ref.5) | copy-start | bytes 1540
  32.2 8.6 %copy-start.4 = (f32[3,4,512]{2,1,0:T(4,128)S(1)}, f32[3,4,512]{2,1,0:T(4,128)}, u32[]{:S(2)}) copy-start(f32[3,4,512]{2,1,0:T(4,128)} %dev_ref.1) | copy-start | bytes 73732

commit v2 on v1

--- a/solution.py
+++ b/solution.py
@@ -121,13 +121,16 @@
     return jnp.concatenate([turned[WIDTH * j : WIDTH * (j + 1)] for j in range(8)], axis=1)
 
 
-def sums_of(slots, rows, states):
-    turned = rows.T.astype(jnp.int32)
-    index = jnp.concatenate([turned[WIDTH * j + 12 : WIDTH * j + 13] for j in range(8)], axis=1)
-    state = lax.broadcasted_iota(jnp.int32, (states, index.shape[1]), 0)
-    hot = jnp.where(state == index, 1.0, 0.0).astype(BF16)
-    both = (((1,), (1,)), ((), ()))
-    return whole(lax.dot_general(split3(slots), hot, both, preferred_element_type=F32))
+def hot_lanes(index, count):
+    lanes = lax.broadcasted_iota(jnp.int32, (index.shape[0], count), 1)
+    return jnp.where(lanes == index, 1.0, 0.0).astype(BF16)
+
+
+def received_hot(rows, count):
+    index = rows.astype(jnp.int32)
+    return jnp.concatenate(
+        [hot_lanes(index[:, WIDTH * j + 12 : WIDTH * j + 13], count) for j in range(8)], axis=0
+    )
 
 
 def zero_kernel(out_ref):
@@ -150,7 +153,8 @@
     senders = index_ref.shape[0]
     depth = rows_ref.shape[0] // senders
     rows = rows_ref[...] if depth == 1 else rows_ref[pl.ds(0, senders, stride=depth), :]
-    packed = pack(sums_of(received_slots(rows), index_ref[...], states))
+    hot = received_hot(index_ref[...], states)
+    packed = pack(whole(jnp.dot(split3(received_slots(rows)), hot, preferred_element_type=F32)))
     for i in range(out_ref.shape[0]):
         out_ref[i] = packed
 
@@ -218,7 +222,10 @@
 
 
 def share(part):
-    return lax.all_to_all(part, "pb", 0, 0, tiled=True)
+    groups = lax.axis_size("pb")
+    orders = [list(range(groups)), [0, *range(groups - 1, 0, -1)]]
+    members = [[groups * pool + x for x in orders[pool % 2]] for pool in range(lax.axis_size("pool"))]
+    return lax.all_to_all(part, ("pool", "pb"), 0, 0, axis_index_groups=members, tiled=True)
 
 
 def local(

time: 69.8 us -> 69.6 us (level)
  no operation moved by 1% of the time
where the time goes in v2:
time: 69.6 us; the launch traced here: 69.3 us
  blocking collectives  64.7 us (93%)
  Pallas kernels  3.08 us (4%)
  local copies, waits for them, and re-layouts  0.81 us (1%)
  between operations  0.72 us (1%)
    all_to_all x2, blocking collectives, exchange(): return lax.all_to_all(x, 'pool', 0, 0, tiled=True).reshape(rows.shape)  49 us
    all_to_all x2, blocking collectives, share(): lax.all_to_all(part, ('pool', 'pb'), 0, 0, axis_index_groups=members, til...  15.6 us
    pallas_call x6, Pallas kernels, call(): pl.pallas_call(kernel, out_shape=out_shape, in_specs=[pl.BlockSpec(memory...  3.08 us

profile of v2, /device:TPU:1, one launch (start us, length us, event | category | flops | bytes accessed | tf_op | source)
XLA Modules:
  0.0 69.3 jit_solution(15302575228200028081)
XLA Ops:
  0.6 0.0 copy-start.1
  0.6 0.0 copy-start
  0.7 0.0 copy-start.2
  0.7 0.0 copy-start.5
  0.7 0.0 copy-start.7
  0.7 0.0 copy-start.3
  0.7 0.0 copy-start.6
  0.7 0.7 copy-done.1
  1.4 0.1 copy-done
  1.5 0.0 copy-done.2
  1.5 0.0 copy-done.5
  1.5 0.0 copy-done.7
  1.5 0.0 copy-done.3
  1.5 0.0 copy-done.6
  1.5 0.6 shard_map.96
  2.1 29.7 %all_to_all.20 = f32[128,1,128]{2,1,0:T(1,128)S(1)} all-to-all(f32[128,1,128]{2,1,0:T(1,128)S(1)} %bitcast.16), channel_id=1, replica_groups=mesh['pool'=128,'pb'=4] {'pool'}, dimensions={0} | all-to-all | bytes 131072 | tf_op jit(solution)/shard_map/all_to_all | solution.py:221
  31.8 0.4 shard_map.97
  32.1 0.0 copy-start.4
  32.2 8.6 %all_to_all.21.parts_ref = f32[4,8,768]{2,1,0:T(8,128)S(1)} all-to-all(f32[4,8,768]{2,1,0:T(8,128)S(1)} %shard_map.97), channel_id=1, replica_groups={{0,1,2,3},{4,7,6,5},{8,9,10,11},{12,15,14,13},{16,17,18,19},{20,23,22,2..., dimensions={0} | all-to-all | bytes 196608 | tf_op jit(solution)/shard_map/all_to_all | solution.py:228
  40.8 0.0 copy-done.4
  40.8 0.6 shard_map.98
  41.4 19.4 %all_to_all.22 = f32[128,2,128]{2,1,0:T(2,128)S(1)} all-to-all(f32[128,2,128]{2,1,0:T(2,128)S(1)} %bitcast.15), channel_id=1, replica_groups=mesh['pool'=128,'pb'=4] {'pool'}, dimensions={0} | all-to-all | bytes 262144 | tf_op jit(solution)/shard_map/all_to_all | solution.py:221
  60.8 0.4 shard_map.99
  61.2 7.0 %all_to_all.23.parts_ref = f32[4,8,768]{2,1,0:T(8,128)S(1)} all-to-all(f32[4,8,768]{2,1,0:T(8,128)S(1)} %shard_map.99), channel_id=1, replica_groups={{0,1,2,3},{4,7,6,5},{8,9,10,11},{12,15,14,13},{16,17,18,19},{20,23,22,2..., dimensions={0} | all-to-all | bytes 196608 | tf_op jit(solution)/shard_map/all_to_all | solution.py:228
  68.2 1.1 %shard_map.100 = (f32[3,4,512]{2,1,0:T(4,128)}, f32[16,1024]{1,0:T(8,128)}) custom-call(f32[4,8,768]{2,1,0:T(8,128)S(1)} %all_to_all.23.parts_ref, f32[256,128]{1,0:T(8,128)S(1)} %bitcast.14, f32[3,4,512]{2,1,0:T(4,128)S(1)} %copy-done.1, f32[4,512]{1,0:T(4,128)S(1)} %copy-done.2, s32[1,512]{1,0:T(1,128)S(1)} %bitcast.22, s32[1,1024]{1,0:T(1,128)S(1)} %bitcast.19, ...), custom_call_target="tpu_custom_call" | custom-call | tf_op jit(solution)/shard_map/pallas_call | solution.py:208
  (1 shorter events, 0.0 us)
Async XLA Ops:
  0.6 0.7 %copy-start.1 = (f32[3,4,512]{2,1,0:T(4,128)S(1)}, f32[3,4,512]{2,1,0:T(4,128)}, u32[]{:S(2)}) copy-start(f32[3,4,512]{2,1,0:T(4,128)} %source_ref.5) | copy-start | bytes 73732
  0.6 0.8 %copy-start = (f32[16,1024]{1,0:T(8,128)S(1)}, f32[16,1024]{1,0:T(8,128)}, u32[]{:S(2)}) copy-start(f32[16,1024]{1,0:T(8,128)} %couple_ref.3) | copy-start | bytes 196612
  0.7 0.8 %copy-start.2 = (f32[4,512]{1,0:T(4,128)S(1)}, f32[4,512]{1,0:T(4,128)}, u32[]{:S(2)}) copy-start(f32[4,512]{1,0:T(4,128)} %relax_ref.5) | copy-start | bytes 24580
  0.7 0.8 %copy-start.5 = (s32[512]{0:T(512)S(1)}, s32[512]{0:T(512)}, u32[]{:S(2)}) copy-start(s32[512]{0:T(512)} %param.11) | copy-start | bytes 6148
  0.7 0.8 %copy-start.7 = (s32[1024]{0:T(1024)S(1)}, s32[1024]{0:T(1024)}, u32[]{:S(2)}) copy-start(s32[1024]{0:T(1024)} %param.13) | copy-start | bytes 12292
  0.7 0.8 %copy-start.3 = (s32[1024]{0:T(1024)S(1)}, s32[1024]{0:T(1024)}, u32[]{:S(2)}) copy-start(s32[1024]{0:T(1024)} %param.12) | copy-start | bytes 12292
  0.7 0.8 %copy-start.6 = (s32[1,128]{1,0:T(1,128)S(1)}, s32[1,128]{1,0:T(1,128)}, u32[]{:S(2)}) copy-start(s32[1,128]{1,0:T(1,128)} %fill_ref.5) | copy-start | bytes 1540
  32.1 8.6 %copy-start.4 = (f32[3,4,512]{2,1,0:T(4,128)S(1)}, f32[3,4,512]{2,1,0:T(4,128)}, u32[]{:S(2)}) copy-start(f32[3,4,512]{2,1,0:T(4,128)} %dev_ref.1) | copy-start | bytes 73732

commit v3 on v1

--- a/solution.py
+++ b/solution.py
@@ -121,13 +121,18 @@
     return jnp.concatenate([turned[WIDTH * j : WIDTH * (j + 1)] for j in range(8)], axis=1)
 
 
-def sums_of(slots, rows, states):
-    turned = rows.T.astype(jnp.int32)
-    index = jnp.concatenate([turned[WIDTH * j + 12 : WIDTH * j + 13] for j in range(8)], axis=1)
-    state = lax.broadcasted_iota(jnp.int32, (states, index.shape[1]), 0)
-    hot = jnp.where(state == index, 1.0, 0.0).astype(BF16)
-    both = (((1,), (1,)), ((), ()))
-    return whole(lax.dot_general(split3(slots), hot, both, preferred_element_type=F32))
+def received_hot(rows, states):
+    width = min(256, states)
+    lane = lax.broadcasted_iota(jnp.int32, (rows.shape[0], width), 1).astype(F32).astype(BF16)
+    blocks = []
+    for j in range(8):
+        column = rows[:, WIDTH * j + 12 : WIDTH * j + 13]
+        parts = [
+            jnp.where((column - first).astype(BF16) == lane, jnp.ones_like(lane), jnp.zeros_like(lane))
+            for first in range(0, states, width)
+        ]
+        blocks.append(jnp.concatenate(parts, axis=1))
+    return jnp.concatenate(blocks, axis=0)
 
 
 def zero_kernel(out_ref):
@@ -150,7 +155,8 @@
     senders = index_ref.shape[0]
     depth = rows_ref.shape[0] // senders
     rows = rows_ref[...] if depth == 1 else rows_ref[pl.ds(0, senders, stride=depth), :]
-    packed = pack(sums_of(received_slots(rows), index_ref[...], states))
+    hot = received_hot(index_ref[...], states)
+    packed = pack(whole(jnp.dot(split3(received_slots(rows)), hot, preferred_element_type=F32)))
     for i in range(out_ref.shape[0]):
         out_ref[i] = packed
 

time: 69.8 us -> 69.6 us (level)
  no operation moved by 1% of the time
where the time goes in v3:
time: 69.6 us; the launch traced here: 69.3 us
  blocking collectives  64.7 us (93%)
  Pallas kernels  3.07 us (4%)
  local copies, waits for them, and re-layouts  0.81 us (1%)
  between operations  0.72 us (1%)
    all_to_all x2, blocking collectives, exchange(): return lax.all_to_all(x, 'pool', 0, 0, tiled=True).reshape(rows.shape)  49 us
    all_to_all x2, blocking collectives, share(): return lax.all_to_all(part, 'pb', 0, 0, tiled=True)  15.6 us
    pallas_call x6, Pallas kernels, call(): pl.pallas_call(kernel, out_shape=out_shape, in_specs=[pl.BlockSpec(memory...  3.07 us

profile of v3, /device:TPU:1, one launch (start us, length us, event | category | flops | bytes accessed | tf_op | source)
XLA Modules:
  0.0 69.3 jit_solution(8300046250255609026)
XLA Ops:
  0.6 0.0 copy-start.1
  0.6 0.0 copy-start
  0.7 0.0 copy-start.2
  0.7 0.0 copy-start.5
  0.7 0.0 copy-start.7
  0.7 0.0 copy-start.3
  0.7 0.0 copy-start.6
  0.7 0.7 copy-done.1
  1.4 0.1 copy-done
  1.5 0.0 copy-done.2
  1.5 0.0 copy-done.5
  1.5 0.0 copy-done.7
  1.5 0.0 copy-done.3
  1.5 0.0 copy-done.6
  1.5 0.6 shard_map.96
  2.1 29.7 %all_to_all.20 = f32[128,1,128]{2,1,0:T(1,128)S(1)} all-to-all(f32[128,1,128]{2,1,0:T(1,128)S(1)} %bitcast.16), channel_id=1, replica_groups=mesh['pool'=128,'pb'=4] {'pool'}, dimensions={0} | all-to-all | bytes 131072 | tf_op jit(solution)/shard_map/all_to_all | solution.py:223
  31.8 0.4 shard_map.97
  32.1 0.0 copy-start.4
  32.1 8.6 %all_to_all.21.parts_ref = f32[4,8,768]{2,1,0:T(8,128)S(1)} all-to-all(f32[4,8,768]{2,1,0:T(8,128)S(1)} %shard_map.97), channel_id=1, replica_groups=mesh['pool'=128,'pb'=4] {'pb'}, dimensions={0} | all-to-all | bytes 196608 | tf_op jit(solution)/shard_map/all_to_all | solution.py:227
  40.8 0.0 copy-done.4
  40.8 0.6 shard_map.98
  41.4 19.4 %all_to_all.22 = f32[128,2,128]{2,1,0:T(2,128)S(1)} all-to-all(f32[128,2,128]{2,1,0:T(2,128)S(1)} %bitcast.15), channel_id=1, replica_groups=mesh['pool'=128,'pb'=4] {'pool'}, dimensions={0} | all-to-all | bytes 262144 | tf_op jit(solution)/shard_map/all_to_all | solution.py:223
  60.8 0.4 shard_map.99
  61.2 7.0 %all_to_all.23.parts_ref = f32[4,8,768]{2,1,0:T(8,128)S(1)} all-to-all(f32[4,8,768]{2,1,0:T(8,128)S(1)} %shard_map.99), channel_id=1, replica_groups=mesh['pool'=128,'pb'=4] {'pb'}, dimensions={0} | all-to-all | bytes 196608 | tf_op jit(solution)/shard_map/all_to_all | solution.py:227
  68.2 1.1 %shard_map.100 = (f32[3,4,512]{2,1,0:T(4,128)}, f32[16,1024]{1,0:T(8,128)}) custom-call(f32[4,8,768]{2,1,0:T(8,128)S(1)} %all_to_all.23.parts_ref, f32[256,128]{1,0:T(8,128)S(1)} %bitcast.14, f32[3,4,512]{2,1,0:T(4,128)S(1)} %copy-done.1, f32[4,512]{1,0:T(4,128)S(1)} %copy-done.2, s32[1,512]{1,0:T(1,128)S(1)} %bitcast.22, s32[1,1024]{1,0:T(1,128)S(1)} %bitcast.19, ...), custom_call_target="tpu_custom_call" | custom-call | tf_op jit(solution)/shard_map/pallas_call | solution.py:210
  (1 shorter events, 0.0 us)
Async XLA Ops:
  0.6 0.7 %copy-start.1 = (f32[3,4,512]{2,1,0:T(4,128)S(1)}, f32[3,4,512]{2,1,0:T(4,128)}, u32[]{:S(2)}) copy-start(f32[3,4,512]{2,1,0:T(4,128)} %source_ref.5) | copy-start | bytes 73732
  0.6 0.8 %copy-start = (f32[16,1024]{1,0:T(8,128)S(1)}, f32[16,1024]{1,0:T(8,128)}, u32[]{:S(2)}) copy-start(f32[16,1024]{1,0:T(8,128)} %couple_ref.3) | copy-start | bytes 196612
  0.7 0.8 %copy-start.2 = (f32[4,512]{1,0:T(4,128)S(1)}, f32[4,512]{1,0:T(4,128)}, u32[]{:S(2)}) copy-start(f32[4,512]{1,0:T(4,128)} %relax_ref.5) | copy-start | bytes 24580
  0.7 0.8 %copy-start.5 = (s32[512]{0:T(512)S(1)}, s32[512]{0:T(512)}, u32[]{:S(2)}) copy-start(s32[512]{0:T(512)} %param.11) | copy-start | bytes 6148
  0.7 0.8 %copy-start.7 = (s32[1024]{0:T(1024)S(1)}, s32[1024]{0:T(1024)}, u32[]{:S(2)}) copy-start(s32[1024]{0:T(1024)} %param.13) | copy-start | bytes 12292
  0.7 0.8 %copy-start.3 = (s32[1024]{0:T(1024)S(1)}, s32[1024]{0:T(1024)}, u32[]{:S(2)}) copy-start(s32[1024]{0:T(1024)} %param.12) | copy-start | bytes 12292
  0.7 0.8 %copy-start.6 = (s32[1,128]{1,0:T(1,128)S(1)}, s32[1,128]{1,0:T(1,128)}, u32[]{:S(2)}) copy-start(s32[1,128]{1,0:T(1,128)} %fill_ref.5) | copy-start | bytes 1540
  32.1 8.6 %copy-start.4 = (f32[3,4,512]{2,1,0:T(4,128)S(1)}, f32[3,4,512]{2,1,0:T(4,128)}, u32[]{:S(2)}) copy-start(f32[3,4,512]{2,1,0:T(4,128)} %dev_ref.1) | copy-start | bytes 73732

commit v4 on v3

--- a/solution.py
+++ b/solution.py
@@ -88,12 +88,19 @@
     return out
 
 
+def tile_rows(x, first):
+    start = first // 8 * 8
+    half = x[start : start + 8]
+    turned = pltpu.roll(half, 4, 0)
+    low = lax.broadcasted_iota(jnp.int32, half.shape, 0) < 4
+    out = jnp.where(low, half, turned) if first == start else jnp.where(low, turned, half)
+    return jnp.concatenate([out, out], axis=0)
+
+
 def scatter_terms(picked, live, couple):
     total = None
     for band in range(4):
-        block = couple[4 * band : 4 * band + 4]
-        block = jnp.concatenate([block, block, block, jnp.zeros_like(block)], axis=0)
-        term = block * repeat_rows(picked, band, 4, 3)
+        term = tile_rows(couple, 4 * band) * repeat_rows(picked, band, 4, 3)
         total = term if total is None else total + term
     return total * live
 
@@ -200,8 +207,7 @@
     picked = select(relax * multiplier, src_ref[...])
     total = None
     for d in range(3):
-        far = fetched[4 * d : 4 * d + 4]
-        term = repeat_rows(picked, 4 * d, 1, 4) * jnp.concatenate([far] * 4, axis=0)
+        term = repeat_rows(picked, 4 * d, 1, 4) * tile_rows(fetched, 4 * d)
         total = term if total is None else total + term
     grad_ref[...] = total * live_row(fill_ref, src_ref.shape[1])
 
@@ -219,7 +225,7 @@
 
 def exchange(rows):
     pools = lax.axis_size("pool")
-    x = rows.reshape(pools, -1, 128)
+    x = rows.reshape(pools, 1, -1)
     return lax.all_to_all(x, "pool", 0, 0, tiled=True).reshape(rows.shape)
 
 

time: 69.6 us -> 69.6 us (level)
  no operation moved by 1% of the time
where the time goes in v4:
time: 69.6 us; the launch traced here: 69.3 us
  blocking collectives  64.7 us (93%)
  Pallas kernels  3.08 us (4%)
  local copies, waits for them, and re-layouts  0.81 us (1%)
  between operations  0.72 us (1%)
    all_to_all x2, blocking collectives, exchange(): return lax.all_to_all(x, 'pool', 0, 0, tiled=True).reshape(rows.shape)  49 us
    all_to_all x2, blocking collectives, share(): return lax.all_to_all(part, 'pb', 0, 0, tiled=True)  15.6 us
    pallas_call x6, Pallas kernels, call(): pl.pallas_call(kernel, out_shape=out_shape, in_specs=[pl.BlockSpec(memory...  3.08 us

profile of v4, /device:TPU:1, one launch (start us, length us, event | category | flops | bytes accessed | tf_op | source)
XLA Modules:
  0.0 69.3 jit_solution(18281594396964407960)
XLA Ops:
  0.6 0.0 copy-start.1
  0.6 0.0 copy-start
  0.7 0.0 copy-start.2
  0.7 0.0 copy-start.5
  0.7 0.0 copy-start.7
  0.7 0.0 copy-start.3
  0.7 0.0 copy-start.6
  0.7 0.7 copy-done.1
  1.4 0.1 copy-done
  1.5 0.0 copy-done.2
  1.5 0.0 copy-done.5
  1.5 0.0 copy-done.7
  1.5 0.0 copy-done.3
  1.5 0.0 copy-done.6
  1.5 0.6 shard_map.96
  2.1 29.7 %all_to_all.20 = f32[128,1,128]{2,1,0:T(1,128)S(1)} all-to-all(f32[128,1,128]{2,1,0:T(1,128)S(1)} %bitcast.16), channel_id=1, replica_groups=mesh['pool'=128,'pb'=4] {'pool'}, dimensions={0} | all-to-all | bytes 131072 | tf_op jit(solution)/shard_map/all_to_all | solution.py:229
  31.8 0.4 shard_map.97
  32.1 0.0 copy-start.4
  32.1 8.6 %all_to_all.21.parts_ref = f32[4,8,768]{2,1,0:T(8,128)S(1)} all-to-all(f32[4,8,768]{2,1,0:T(8,128)S(1)} %shard_map.97), channel_id=1, replica_groups=mesh['pool'=128,'pb'=4] {'pb'}, dimensions={0} | all-to-all | bytes 196608 | tf_op jit(solution)/shard_map/all_to_all | solution.py:233
  40.8 0.0 copy-done.4
  40.8 0.6 shard_map.98
  41.4 19.4 %all_to_all.22 = f32[128,1,256]{2,1,0:T(1,128)S(1)} all-to-all(f32[128,1,256]{2,1,0:T(1,128)S(1)} %bitcast.15), channel_id=1, replica_groups=mesh['pool'=128,'pb'=4] {'pool'}, dimensions={0} | all-to-all | bytes 262144 | tf_op jit(solution)/shard_map/all_to_all | solution.py:229
  60.8 0.4 shard_map.99
  61.2 7.0 %all_to_all.23.parts_ref = f32[4,8,768]{2,1,0:T(8,128)S(1)} all-to-all(f32[4,8,768]{2,1,0:T(8,128)S(1)} %shard_map.99), channel_id=1, replica_groups=mesh['pool'=128,'pb'=4] {'pb'}, dimensions={0} | all-to-all | bytes 196608 | tf_op jit(solution)/shard_map/all_to_all | solution.py:233
  68.2 1.1 %shard_map.100 = (f32[3,4,512]{2,1,0:T(4,128)}, f32[16,1024]{1,0:T(8,128)}) custom-call(f32[4,8,768]{2,1,0:T(8,128)S(1)} %all_to_all.23.parts_ref, f32[256,128]{1,0:T(8,128)S(1)} %bitcast.14, f32[3,4,512]{2,1,0:T(4,128)S(1)} %copy-done.1, f32[4,512]{1,0:T(4,128)S(1)} %copy-done.2, s32[1,512]{1,0:T(1,128)S(1)} %bitcast.22, s32[1,1024]{1,0:T(1,128)S(1)} %bitcast.19, ...), custom_call_target="tpu_custom_call" | custom-call | tf_op jit(solution)/shard_map/pallas_call | solution.py:216
  (1 shorter events, 0.0 us)
Async XLA Ops:
  0.6 0.7 %copy-start.1 = (f32[3,4,512]{2,1,0:T(4,128)S(1)}, f32[3,4,512]{2,1,0:T(4,128)}, u32[]{:S(2)}) copy-start(f32[3,4,512]{2,1,0:T(4,128)} %source_ref.5) | copy-start | bytes 73732
  0.6 0.8 %copy-start = (f32[16,1024]{1,0:T(8,128)S(1)}, f32[16,1024]{1,0:T(8,128)}, u32[]{:S(2)}) copy-start(f32[16,1024]{1,0:T(8,128)} %couple_ref.3) | copy-start | bytes 196612
  0.7 0.8 %copy-start.2 = (f32[4,512]{1,0:T(4,128)S(1)}, f32[4,512]{1,0:T(4,128)}, u32[]{:S(2)}) copy-start(f32[4,512]{1,0:T(4,128)} %relax_ref.5) | copy-start | bytes 24580
  0.7 0.8 %copy-start.5 = (s32[512]{0:T(512)S(1)}, s32[512]{0:T(512)}, u32[]{:S(2)}) copy-start(s32[512]{0:T(512)} %param.11) | copy-start | bytes 6148
  0.7 0.8 %copy-start.7 = (s32[1024]{0:T(1024)S(1)}, s32[1024]{0:T(1024)}, u32[]{:S(2)}) copy-start(s32[1024]{0:T(1024)} %param.13) | copy-start | bytes 12292
  0.7 0.8 %copy-start.3 = (s32[1024]{0:T(1024)S(1)}, s32[1024]{0:T(1024)}, u32[]{:S(2)}) copy-start(s32[1024]{0:T(1024)} %param.12) | copy-start | bytes 12292
  0.7 0.8 %copy-start.6 = (s32[1,128]{1,0:T(1,128)S(1)}, s32[1,128]{1,0:T(1,128)}, u32[]{:S(2)}) copy-start(s32[1,128]{1,0:T(1,128)} %fill_ref.5) | copy-start | bytes 1540
  32.1 8.6 %copy-start.4 = (f32[3,4,512]{2,1,0:T(4,128)S(1)}, f32[3,4,512]{2,1,0:T(4,128)}, u32[]{:S(2)}) copy-start(f32[3,4,512]{2,1,0:T(4,128)} %dev_ref.1) | copy-start | bytes 73732

commit v5 on v3

--- a/solution.py
+++ b/solution.py
@@ -104,6 +104,14 @@
     return jnp.concatenate([flat_ref[pl.ds(j, owners, stride=8), :] for j in range(8)], axis=1)
 
 
+def first_member(pools):
+    return pools * 13 // 16
+
+
+def rotate(rows, start):
+    return jnp.concatenate([rows[start:], rows[:start]], axis=0)
+
+
 def pack(x):
     half = x.shape[1] // 2
     tail = jnp.concatenate([x[8:12, :half], x[8:12, half:]], axis=0)
@@ -148,7 +156,7 @@
     terms = scatter_terms(pick(moment, src_ref[...]), live, couple_ref[...])
     row = lax.broadcasted_iota(jnp.int32, terms.shape, 0)
     terms = jnp.where(row == 12, dst_ref[...].astype(F32) + zero_ref[:1, :1], terms)
-    out_ref[...] = slots_to_rows(terms, flat_ref)
+    out_ref[...] = rotate(slots_to_rows(terms, flat_ref), first_member(out_ref.shape[0]))
 
 
 def gather_kernel(rows_ref, index_ref, out_ref, *, states):
@@ -182,14 +190,15 @@
     moment = relax * multiplier_of(parts_ref, source_ref, window_ref)
     live = live_row(fill_ref, src_ref.shape[1])
     terms = scatter_terms(select(moment, src_ref[...]), live, couple_ref[...])
-    out_ref[pl.ds(0, senders, stride=2), :] = slots_to_rows(terms, flat_ref)
+    rows = rotate(slots_to_rows(terms, flat_ref), first_member(senders))
+    out_ref[pl.ds(0, senders, stride=2), :] = rows
 
 
 def last_kernel(
     parts_ref, rows_ref, source_ref, relax_ref, window_ref, src_ref, fill_ref, multiplier_ref, grad_ref, flat_ref
 ):
     owners = rows_ref.shape[0] // 2
-    rows = rows_ref[pl.ds(1, owners, stride=2), :]
+    rows = rotate(rows_ref[pl.ds(1, owners, stride=2), :], owners - first_member(owners))
     for j in range(8):
         flat_ref[pl.ds(j, owners, stride=8), :] = rows[:, WIDTH * j : WIDTH * (j + 1)]
     fetched = flat_ref[...].T
@@ -219,8 +228,10 @@
 
 def exchange(rows):
     pools = lax.axis_size("pool")
+    members = [[(place + first_member(pools)) % pools for place in range(pools)]]
     x = rows.reshape(pools, -1, 128)
-    return lax.all_to_all(x, "pool", 0, 0, tiled=True).reshape(rows.shape)
+    x = lax.all_to_all(x, "pool", 0, 0, axis_index_groups=members, tiled=True)
+    return x.reshape(rows.shape)
 
 
 def share(part):

time: 69.6 us -> 64.8 us (0.931)
  blocking collectives: 64.7 us -> 59.8 us
    all_to_all x2, blocking collectives: 49 us -> 44.2 us  [exchange(): x = lax.all_to_all(x, 'pool', 0, 0, axis_index_groups=members, tiled=True)]
where the time goes in v5:
time: 64.8 us; the launch traced here: 64.4 us
  blocking collectives  59.8 us (92%)
  Pallas kernels  3.07 us (5%)
  local copies, waits for them, and re-layouts  0.81 us (1%)
  between operations  0.72 us (1%)
    all_to_all x2, blocking collectives, exchange(): x = lax.all_to_all(x, 'pool', 0, 0, axis_index_groups=members, tiled=True)  44.2 us
    all_to_all x2, blocking collectives, share(): return lax.all_to_all(part, 'pb', 0, 0, tiled=True)  15.6 us
    pallas_call x6, Pallas kernels, call(): pl.pallas_call(kernel, out_shape=out_shape, in_specs=[pl.BlockSpec(memory...  3.07 us

profile of v5, /device:TPU:1, one launch (start us, length us, event | category | flops | bytes accessed | tf_op | source)
XLA Modules:
  0.0 64.4 jit_solution(7051040395655313981)
XLA Ops:
  0.6 0.0 copy-start.1
  0.6 0.0 copy-start
  0.7 0.0 copy-start.2
  0.7 0.0 copy-start.5
  0.7 0.0 copy-start.7
  0.7 0.0 copy-start.3
  0.7 0.0 copy-start.6
  0.7 0.7 %copy-done.1 = f32[3,4,512]{2,1,0:T(4,128)S(1)} copy-done((f32[3,4,512]{2,1,0:T(4,128)S(1)}, f32[3,4,512]{2,1,0:T(4,128)}, u32[]{:S(2)}) %copy-start.1) | copy-done | bytes 24600
  1.4 0.1 copy-done
  1.5 0.0 copy-done.2
  1.5 0.0 copy-done.5
  1.5 0.0 copy-done.7
  1.5 0.0 copy-done.3
  1.5 0.0 copy-done.6
  1.5 0.6 shard_map.96
  2.1 24.4 %all_to_all.20 = f32[128,1,128]{2,1,0:T(1,128)S(1)} all-to-all(f32[128,1,128]{2,1,0:T(1,128)S(1)} %bitcast.16), channel_id=1, replica_groups={{416,420,424,428,432,436,440,444,448,452,456,460,464,468,472,476,480,48..., dimensions={0} | all-to-all | bytes 131072 | tf_op jit(solution)/shard_map/all_to_all | solution.py:233
  26.5 0.4 shard_map.97
  26.8 0.0 copy-start.4
  26.9 8.6 %all_to_all.21.parts_ref = f32[4,8,768]{2,1,0:T(8,128)S(1)} all-to-all(f32[4,8,768]{2,1,0:T(8,128)S(1)} %shard_map.97), channel_id=1, replica_groups=mesh['pool'=128,'pb'=4] {'pb'}, dimensions={0} | all-to-all | bytes 196608 | tf_op jit(solution)/shard_map/all_to_all | solution.py:238
  35.5 0.0 copy-done.4
  35.5 0.6 shard_map.98
  36.1 19.8 %all_to_all.22 = f32[128,2,128]{2,1,0:T(2,128)S(1)} all-to-all(f32[128,2,128]{2,1,0:T(2,128)S(1)} %bitcast.15), channel_id=1, replica_groups={{416,420,424,428,432,436,440,444,448,452,456,460,464,468,472,476,480,48..., dimensions={0} | all-to-all | bytes 262144 | tf_op jit(solution)/shard_map/all_to_all | solution.py:233
  55.9 0.4 shard_map.99
  56.3 7.0 %all_to_all.23.parts_ref = f32[4,8,768]{2,1,0:T(8,128)S(1)} all-to-all(f32[4,8,768]{2,1,0:T(8,128)S(1)} %shard_map.99), channel_id=1, replica_groups=mesh['pool'=128,'pb'=4] {'pb'}, dimensions={0} | all-to-all | bytes 196608 | tf_op jit(solution)/shard_map/all_to_all | solution.py:238
  63.4 1.1 %shard_map.100 = (f32[3,4,512]{2,1,0:T(4,128)}, f32[16,1024]{1,0:T(8,128)}) custom-call(f32[4,8,768]{2,1,0:T(8,128)S(1)} %all_to_all.23.parts_ref, f32[256,128]{1,0:T(8,128)S(1)} %bitcast.14, f32[3,4,512]{2,1,0:T(4,128)S(1)} %copy-done.1, f32[4,512]{1,0:T(4,128)S(1)} %copy-done.2, s32[1,512]{1,0:T(1,128)S(1)} %bitcast.22, s32[1,1024]{1,0:T(1,128)S(1)} %bitcast.19, ...), custom_call_target="tpu_custom_call" | custom-call | tf_op jit(solution)/shard_map/pallas_call | solution.py:219
  (1 shorter events, 0.0 us)
Async XLA Ops:
  0.6 0.7 %copy-start.1 = (f32[3,4,512]{2,1,0:T(4,128)S(1)}, f32[3,4,512]{2,1,0:T(4,128)}, u32[]{:S(2)}) copy-start(f32[3,4,512]{2,1,0:T(4,128)} %source_ref.5) | copy-start | bytes 73732
  0.6 0.8 %copy-start = (f32[16,1024]{1,0:T(8,128)S(1)}, f32[16,1024]{1,0:T(8,128)}, u32[]{:S(2)}) copy-start(f32[16,1024]{1,0:T(8,128)} %couple_ref.3) | copy-start | bytes 196612
  0.7 0.8 %copy-start.2 = (f32[4,512]{1,0:T(4,128)S(1)}, f32[4,512]{1,0:T(4,128)}, u32[]{:S(2)}) copy-start(f32[4,512]{1,0:T(4,128)} %relax_ref.5) | copy-start | bytes 24580
  0.7 0.8 %copy-start.5 = (s32[512]{0:T(512)S(1)}, s32[512]{0:T(512)}, u32[]{:S(2)}) copy-start(s32[512]{0:T(512)} %param.11) | copy-start | bytes 6148
  0.7 0.8 %copy-start.7 = (s32[1024]{0:T(1024)S(1)}, s32[1024]{0:T(1024)}, u32[]{:S(2)}) copy-start(s32[1024]{0:T(1024)} %param.13) | copy-start | bytes 12292
  0.7 0.8 %copy-start.3 = (s32[1024]{0:T(1024)S(1)}, s32[1024]{0:T(1024)}, u32[]{:S(2)}) copy-start(s32[1024]{0:T(1024)} %param.12) | copy-start | bytes 12292
  0.7 0.8 %copy-start.6 = (s32[1,128]{1,0:T(1,128)S(1)}, s32[1,128]{1,0:T(1,128)}, u32[]{:S(2)}) copy-start(s32[1,128]{1,0:T(1,128)} %fill_ref.5) | copy-start | bytes 1540
  26.8 8.6 %copy-start.4 = (f32[3,4,512]{2,1,0:T(4,128)S(1)}, f32[3,4,512]{2,1,0:T(4,128)}, u32[]{:S(2)}) copy-start(f32[3,4,512]{2,1,0:T(4,128)} %dev_ref.1) | copy-start | bytes 73732

commit v6 on v3

--- a/solution.py
+++ b/solution.py
@@ -104,6 +104,20 @@
     return jnp.concatenate([flat_ref[pl.ds(j, owners, stride=8), :] for j in range(8)], axis=1)
 
 
+def first_chip(pools):
+    return pools * 13 // 16
+
+
+def to_places(rows):
+    start = first_chip(rows.shape[0])
+    return jnp.concatenate([rows[start + 1 : start + 2], rows[start : start + 1], rows[start + 2 :], rows[:start]], axis=0)
+
+
+def from_places(rows):
+    rest = rows.shape[0] - first_chip(rows.shape[0])
+    return jnp.concatenate([rows[rest:], rows[1:2], rows[:1], rows[2:rest]], axis=0)
+
+
 def pack(x):
     half = x.shape[1] // 2
     tail = jnp.concatenate([x[8:12, :half], x[8:12, half:]], axis=0)
@@ -148,7 +162,7 @@
     terms = scatter_terms(pick(moment, src_ref[...]), live, couple_ref[...])
     row = lax.broadcasted_iota(jnp.int32, terms.shape, 0)
     terms = jnp.where(row == 12, dst_ref[...].astype(F32) + zero_ref[:1, :1], terms)
-    out_ref[...] = slots_to_rows(terms, flat_ref)
+    out_ref[...] = to_places(slots_to_rows(terms, flat_ref))
 
 
 def gather_kernel(rows_ref, index_ref, out_ref, *, states):
@@ -182,14 +196,15 @@
     moment = relax * multiplier_of(parts_ref, source_ref, window_ref)
     live = live_row(fill_ref, src_ref.shape[1])
     terms = scatter_terms(select(moment, src_ref[...]), live, couple_ref[...])
-    out_ref[pl.ds(0, senders, stride=2), :] = slots_to_rows(terms, flat_ref)
+    rows = to_places(slots_to_rows(terms, flat_ref))
+    out_ref[pl.ds(0, senders, stride=2), :] = rows
 
 
 def last_kernel(
     parts_ref, rows_ref, source_ref, relax_ref, window_ref, src_ref, fill_ref, multiplier_ref, grad_ref, flat_ref
 ):
     owners = rows_ref.shape[0] // 2
-    rows = rows_ref[pl.ds(1, owners, stride=2), :]
+    rows = from_places(rows_ref[pl.ds(1, owners, stride=2), :])
     for j in range(8):
         flat_ref[pl.ds(j, owners, stride=8), :] = rows[:, WIDTH * j : WIDTH * (j + 1)]
     fetched = flat_ref[...].T
@@ -219,12 +234,17 @@
 
 def exchange(rows):
     pools = lax.axis_size("pool")
+    members = [(place + first_chip(pools)) % pools for place in range(pools)]
+    members[:2] = members[1::-1]
     x = rows.reshape(pools, -1, 128)
-    return lax.all_to_all(x, "pool", 0, 0, tiled=True).reshape(rows.shape)
+    x = lax.all_to_all(x, "pool", 0, 0, axis_index_groups=[members], tiled=True)
+    return x.reshape(rows.shape)
 
 
 def share(part):
-    return lax.all_to_all(part, "pb", 0, 0, tiled=True)
+    groups = lax.axis_size("pb")
+    members = [(place + groups // 2) % groups for place in range(groups)]
+    return lax.all_to_all(part, "pb", 0, 0, axis_index_groups=[members], tiled=True)
 
 
 def local(

time: 69.6 us -> 61.9 us (0.89)
  blocking collectives: 64.7 us -> 56.9 us
    all_to_all x4, blocking collectives: 64.7 us -> 56.9 us  [the longest x2 42.1 us: exchange(): x = lax.all_to_all(x, 'pool', 0, 0, axis_index_groups=[members], tiled=True)]
where the time goes in v6:
time: 61.9 us; the launch traced here: 61.5 us
  blocking collectives  56.9 us (92%)
  Pallas kernels  3.07 us (5%)
  local copies, waits for them, and re-layouts  0.81 us (1%)
  between operations  0.72 us (1%)
    all_to_all x2, blocking collectives, exchange(): x = lax.all_to_all(x, 'pool', 0, 0, axis_index_groups=[members], tiled=True)  42.1 us
    all_to_all x2, blocking collectives, share(): lax.all_to_all(part, 'pb', 0, 0, axis_index_groups=[members], tiled=True)  14.8 us
    pallas_call x6, Pallas kernels, call(): pl.pallas_call(kernel, out_shape=out_shape, in_specs=[pl.BlockSpec(memory...  3.07 us

profile of v6, /device:TPU:1, one launch (start us, length us, event | category | flops | bytes accessed | tf_op | source)
XLA Modules:
  0.0 61.5 jit_solution(7355824368853566948)
XLA Ops:
  0.6 0.0 copy-start.1
  0.6 0.0 copy-start
  0.7 0.0 copy-start.2
  0.7 0.0 copy-start.5
  0.7 0.0 copy-start.7
  0.7 0.0 copy-start.3
  0.7 0.0 copy-start.6
  0.7 0.7 %copy-done.1 = f32[3,4,512]{2,1,0:T(4,128)S(1)} copy-done((f32[3,4,512]{2,1,0:T(4,128)S(1)}, f32[3,4,512]{2,1,0:T(4,128)}, u32[]{:S(2)}) %copy-start.1) | copy-done | bytes 24600
  1.4 0.1 copy-done
  1.5 0.0 copy-done.2
  1.5 0.0 copy-done.5
  1.5 0.0 copy-done.7
  1.5 0.0 copy-done.3
  1.5 0.0 copy-done.6
  1.5 0.6 shard_map.96
  2.1 23.8 %all_to_all.20 = f32[128,1,128]{2,1,0:T(1,128)S(1)} all-to-all(f32[128,1,128]{2,1,0:T(1,128)S(1)} %bitcast.16), channel_id=1, replica_groups={{420,416,424,428,432,436,440,444,448,452,456,460,464,468,472,476,480,48..., dimensions={0} | all-to-all | bytes 131072 | tf_op jit(solution)/shard_map/all_to_all | solution.py:240
  25.9 0.4 shard_map.97
  26.3 0.0 copy-start.4
  26.3 7.2 %all_to_all.21.parts_ref = f32[4,8,768]{2,1,0:T(8,128)S(1)} all-to-all(f32[4,8,768]{2,1,0:T(8,128)S(1)} %shard_map.97), channel_id=1, replica_groups={{2,3,0,1},{6,7,4,5},{10,11,8,9},{14,15,12,13},{18,19,16,17},{22,23,20,2..., dimensions={0} | all-to-all | bytes 196608 | tf_op jit(solution)/shard_map/all_to_all | solution.py:247
  33.5 0.0 copy-done.4
  33.5 0.6 %shard_map.98 = f32[256,128]{1,0:T(8,128)S(1)} custom-call(f32[4,8,768]{2,1,0:T(8,128)S(1)} %all_to_all.21.parts_ref, f32[128,128]{1,0:T(8,128)S(1)} %bitcast.11, f32[3,4,512]{2,1,0:T(4,128)S(1)} %copy-done.4, f32[3,4,512]{2,1,0:T(4,128)S(1)} %copy-done.1, f32[4,512]{1,0:T(4,128)S(1)} %copy-done.2, s32[1,512]{1,0:T(1,128)S(1)} %bitcast.21, ...), custom_call_target="tpu_custom_call" | custom-call | tf_op jit(solution)/shard_map/pallas_call | solution.py:225
  34.2 18.3 %all_to_all.22 = f32[128,2,128]{2,1,0:T(2,128)S(1)} all-to-all(f32[128,2,128]{2,1,0:T(2,128)S(1)} %bitcast.15), channel_id=1, replica_groups={{420,416,424,428,432,436,440,444,448,452,456,460,464,468,472,476,480,48..., dimensions={0} | all-to-all | bytes 262144 | tf_op jit(solution)/shard_map/all_to_all | solution.py:240
  52.5 0.4 shard_map.99
  52.9 7.6 %all_to_all.23.parts_ref = f32[4,8,768]{2,1,0:T(8,128)S(1)} all-to-all(f32[4,8,768]{2,1,0:T(8,128)S(1)} %shard_map.99), channel_id=1, replica_groups={{2,3,0,1},{6,7,4,5},{10,11,8,9},{14,15,12,13},{18,19,16,17},{22,23,20,2..., dimensions={0} | all-to-all | bytes 196608 | tf_op jit(solution)/shard_map/all_to_all | solution.py:247
  60.4 1.1 %shard_map.100 = (f32[3,4,512]{2,1,0:T(4,128)}, f32[16,1024]{1,0:T(8,128)}) custom-call(f32[4,8,768]{2,1,0:T(8,128)S(1)} %all_to_all.23.parts_ref, f32[256,128]{1,0:T(8,128)S(1)} %bitcast.14, f32[3,4,512]{2,1,0:T(4,128)S(1)} %copy-done.1, f32[4,512]{1,0:T(4,128)S(1)} %copy-done.2, s32[1,512]{1,0:T(1,128)S(1)} %bitcast.22, s32[1,1024]{1,0:T(1,128)S(1)} %bitcast.19, ...), custom_call_target="tpu_custom_call" | custom-call | tf_op jit(solution)/shard_map/pallas_call | solution.py:225
  (1 shorter events, 0.0 us)
Async XLA Ops:
  0.6 0.7 %copy-start.1 = (f32[3,4,512]{2,1,0:T(4,128)S(1)}, f32[3,4,512]{2,1,0:T(4,128)}, u32[]{:S(2)}) copy-start(f32[3,4,512]{2,1,0:T(4,128)} %source_ref.5) | copy-start | bytes 73732
  0.6 0.8 %copy-start = (f32[16,1024]{1,0:T(8,128)S(1)}, f32[16,1024]{1,0:T(8,128)}, u32[]{:S(2)}) copy-start(f32[16,1024]{1,0:T(8,128)} %couple_ref.3) | copy-start | bytes 196612
  0.7 0.8 %copy-start.2 = (f32[4,512]{1,0:T(4,128)S(1)}, f32[4,512]{1,0:T(4,128)}, u32[]{:S(2)}) copy-start(f32[4,512]{1,0:T(4,128)} %relax_ref.5) | copy-start | bytes 24580
  0.7 0.8 %copy-start.5 = (s32[512]{0:T(512)S(1)}, s32[512]{0:T(512)}, u32[]{:S(2)}) copy-start(s32[512]{0:T(512)} %param.11) | copy-start | bytes 6148
  0.7 0.8 %copy-start.7 = (s32[1024]{0:T(1024)S(1)}, s32[1024]{0:T(1024)}, u32[]{:S(2)}) copy-start(s32[1024]{0:T(1024)} %param.13) | copy-start | bytes 12292
  0.7 0.8 %copy-start.3 = (s32[1024]{0:T(1024)S(1)}, s32[1024]{0:T(1024)}, u32[]{:S(2)}) copy-start(s32[1024]{0:T(1024)} %param.12) | copy-start | bytes 12292
  0.7 0.8 %copy-start.6 = (s32[1,128]{1,0:T(1,128)S(1)}, s32[1,128]{1,0:T(1,128)}, u32[]{:S(2)}) copy-start(s32[1,128]{1,0:T(1,128)} %fill_ref.5) | copy-start | bytes 1540
  26.3 7.2 %copy-start.4 = (f32[3,4,512]{2,1,0:T(4,128)S(1)}, f32[3,4,512]{2,1,0:T(4,128)}, u32[]{:S(2)}) copy-start(f32[3,4,512]{2,1,0:T(4,128)} %dev_ref.1) | copy-start | bytes 73732

commit v7 on v6

--- a/solution.py
+++ b/solution.py
@@ -104,17 +104,16 @@
     return jnp.concatenate([flat_ref[pl.ds(j, owners, stride=8), :] for j in range(8)], axis=1)
 
 
-def first_chip(pools):
-    return pools * 13 // 16
-
-
-def to_places(rows):
-    start = first_chip(rows.shape[0])
+FIRST, SECOND = 13, 9
+
+
+def to_places(rows, at):
+    start = rows.shape[0] * at // 16
     return jnp.concatenate([rows[start + 1 : start + 2], rows[start : start + 1], rows[start + 2 :], rows[:start]], axis=0)
 
 
-def from_places(rows):
-    rest = rows.shape[0] - first_chip(rows.shape[0])
+def from_places(rows, at):
+    rest = rows.shape[0] - rows.shape[0] * at // 16
     return jnp.concatenate([rows[rest:], rows[1:2], rows[:1], rows[2:rest]], axis=0)
 
 
@@ -162,14 +161,17 @@
     terms = scatter_terms(pick(moment, src_ref[...]), live, couple_ref[...])
     row = lax.broadcasted_iota(jnp.int32, terms.shape, 0)
     terms = jnp.where(row == 12, dst_ref[...].astype(F32) + zero_ref[:1, :1], terms)
-    out_ref[...] = to_places(slots_to_rows(terms, flat_ref))
+    out_ref[...] = to_places(slots_to_rows(terms, flat_ref), FIRST)
 
 
 def gather_kernel(rows_ref, index_ref, out_ref, *, states):
     senders = index_ref.shape[0]
     depth = rows_ref.shape[0] // senders
-    rows = rows_ref[...] if depth == 1 else rows_ref[pl.ds(0, senders, stride=depth), :]
-    hot = received_hot(index_ref[...], states)
+    rows, index = rows_ref[...], index_ref[...]
+    if depth > 1:
+        rows = rows_ref[pl.ds(0, senders, stride=depth), :]
+        index = to_places(from_places(index, FIRST), SECOND)
+    hot = received_hot(index, states)
     packed = pack(whole(jnp.dot(split3(received_slots(rows)), hot, preferred_element_type=F32)))
     for i in range(out_ref.shape[0]):
         out_ref[i] = packed
@@ -191,12 +193,13 @@
     parts_ref, index_ref, dev_ref, source_ref, relax_ref, window_ref, src_ref, fill_ref, couple_ref, out_ref, flat_ref
 ):
     senders = index_ref.shape[0]
-    out_ref[pl.ds(1, senders, stride=2), :] = returned_rows(dev_ref, window_ref, index_ref)
+    back = returned_rows(dev_ref, window_ref, index_ref)
+    out_ref[pl.ds(1, senders, stride=2), :] = to_places(from_places(back, FIRST), SECOND)
     relax = jnp.concatenate([relax_ref[...]] * 4, axis=0)
     moment = relax * multiplier_of(parts_ref, source_ref, window_ref)
     live = live_row(fill_ref, src_ref.shape[1])
     terms = scatter_terms(select(moment, src_ref[...]), live, couple_ref[...])
-    rows = to_places(slots_to_rows(terms, flat_ref))
+    rows = to_places(slots_to_rows(terms, flat_ref), SECOND)
     out_ref[pl.ds(0, senders, stride=2), :] = rows
 
 
@@ -204,7 +207,7 @@
     parts_ref, rows_ref, source_ref, relax_ref, window_ref, src_ref, fill_ref, multiplier_ref, grad_ref, flat_ref
 ):
     owners = rows_ref.shape[0] // 2
-    rows = from_places(rows_ref[pl.ds(1, owners, stride=2), :])
+    rows = from_places(rows_ref[pl.ds(1, owners, stride=2), :], SECOND)
     for j in range(8):
         flat_ref[pl.ds(j, owners, stride=8), :] = rows[:, WIDTH * j : WIDTH * (j + 1)]
     fetched = flat_ref[...].T
@@ -232,9 +235,9 @@
     )(*operands)
 
 
-def exchange(rows):
+def exchange(rows, at):
     pools = lax.axis_size("pool")
-    members = [(place + first_chip(pools)) % pools for place in range(pools)]
+    members = [(place + pools * at // 16) % pools for place in range(pools)]
     members[:2] = members[1::-1]
     x = rows.reshape(pools, -1, 128)
     x = lax.all_to_all(x, "pool", 0, 0, axis_index_groups=[members], tiled=True)
@@ -266,14 +269,14 @@
         first_kernel, sds((pools, 128), F32), [flat],
         zero, coupling, adjoint_source, relax_time, window, src, dst, bucket_fill,
     )
-    index = exchange(sent)
+    index = exchange(sent, FIRST)
     gather = functools.partial(gather_kernel, states=states)
     parts = share(call(gather, partial, [], index, index))
     sent = call(
         second_kernel, sds((2 * pools, 128), F32), [flat],
         parts, index, deviation, adjoint_source, relax_time, window, src, bucket_fill, coupling,
     )
-    rows = exchange(sent)
+    rows = exchange(sent, SECOND)
     parts = share(call(gather, partial, [], rows, index))
     return call(
         last_kernel, (sds(adjoint_source.shape, F32), sds(coupling.shape, F32)), [flat],

time: 61.9 us -> 61.8 us (level)
  no operation moved by 1% of the time
where the time goes in v7:
time: 61.8 us; the launch traced here: 61.5 us
  blocking collectives  56.9 us (92%)
  Pallas kernels  3.07 us (5%)
  local copies, waits for them, and re-layouts  0.81 us (1%)
  between operations  0.72 us (1%)
    all_to_all x2, blocking collectives, exchange(): x = lax.all_to_all(x, 'pool', 0, 0, axis_index_groups=[members], tiled=True)  42.1 us
    all_to_all x2, blocking collectives, share(): lax.all_to_all(part, 'pb', 0, 0, axis_index_groups=[members], tiled=True)  14.8 us
    pallas_call x6, Pallas kernels, call(): pl.pallas_call(kernel, out_shape=out_shape, in_specs=[pl.BlockSpec(memory...  3.07 us

profile of v7, /device:TPU:1, one launch (start us, length us, event | category | flops | bytes accessed | tf_op | source)
XLA Modules:
  0.0 61.5 jit_solution(15575452474674165400)
XLA Ops:
  0.6 0.0 copy-start.1
  0.6 0.0 copy-start
  0.7 0.0 copy-start.2
  0.7 0.0 copy-start.5
  0.7 0.0 copy-start.7
  0.7 0.0 copy-start.3
  0.7 0.0 copy-start.6
  0.7 0.7 %copy-done.1 = f32[3,4,512]{2,1,0:T(4,128)S(1)} copy-done((f32[3,4,512]{2,1,0:T(4,128)S(1)}, f32[3,4,512]{2,1,0:T(4,128)}, u32[]{:S(2)}) %copy-start.1) | copy-done | bytes 24600
  1.4 0.1 copy-done
  1.5 0.0 copy-done.2
  1.5 0.0 copy-done.5
  1.5 0.0 copy-done.7
  1.5 0.0 copy-done.3
  1.5 0.0 copy-done.6
  1.5 0.6 shard_map.96
  2.1 23.8 %all_to_all.20 = f32[128,1,128]{2,1,0:T(1,128)S(1)} all-to-all(f32[128,1,128]{2,1,0:T(1,128)S(1)} %bitcast.16), channel_id=1, replica_groups={{420,416,424,428,432,436,440,444,448,452,456,460,464,468,472,476,480,48..., dimensions={0} | all-to-all | bytes 131072 | tf_op jit(solution)/shard_map/all_to_all | solution.py:243
  25.9 0.4 shard_map.97
  26.3 0.0 copy-start.4
  26.3 7.2 %all_to_all.21.parts_ref = f32[4,8,768]{2,1,0:T(8,128)S(1)} all-to-all(f32[4,8,768]{2,1,0:T(8,128)S(1)} %shard_map.97), channel_id=1, replica_groups={{2,3,0,1},{6,7,4,5},{10,11,8,9},{14,15,12,13},{18,19,16,17},{22,23,20,2..., dimensions={0} | all-to-all | bytes 196608 | tf_op jit(solution)/shard_map/all_to_all | solution.py:250
  33.5 0.0 copy-done.4
  33.5 0.6 %shard_map.98 = f32[256,128]{1,0:T(8,128)S(1)} custom-call(f32[4,8,768]{2,1,0:T(8,128)S(1)} %all_to_all.21.parts_ref, f32[128,128]{1,0:T(8,128)S(1)} %bitcast.11, f32[3,4,512]{2,1,0:T(4,128)S(1)} %copy-done.4, f32[3,4,512]{2,1,0:T(4,128)S(1)} %copy-done.1, f32[4,512]{1,0:T(4,128)S(1)} %copy-done.2, s32[1,512]{1,0:T(1,128)S(1)} %bitcast.21, ...), custom_call_target="tpu_custom_call" | custom-call | tf_op jit(solution)/shard_map/pallas_call | solution.py:228
  34.2 18.3 %all_to_all.22 = f32[128,2,128]{2,1,0:T(2,128)S(1)} all-to-all(f32[128,2,128]{2,1,0:T(2,128)S(1)} %bitcast.15), channel_id=1, replica_groups={{292,288,296,300,304,308,312,316,320,324,328,332,336,340,344,348,352,35..., dimensions={0} | all-to-all | bytes 262144 | tf_op jit(solution)/shard_map/all_to_all | solution.py:243
  52.4 0.4 shard_map.99
  52.8 7.6 %all_to_all.23.parts_ref = f32[4,8,768]{2,1,0:T(8,128)S(1)} all-to-all(f32[4,8,768]{2,1,0:T(8,128)S(1)} %shard_map.99), channel_id=1, replica_groups={{2,3,0,1},{6,7,4,5},{10,11,8,9},{14,15,12,13},{18,19,16,17},{22,23,20,2..., dimensions={0} | all-to-all | bytes 196608 | tf_op jit(solution)/shard_map/all_to_all | solution.py:250
  60.4 1.1 %shard_map.100 = (f32[3,4,512]{2,1,0:T(4,128)}, f32[16,1024]{1,0:T(8,128)}) custom-call(f32[4,8,768]{2,1,0:T(8,128)S(1)} %all_to_all.23.parts_ref, f32[256,128]{1,0:T(8,128)S(1)} %bitcast.14, f32[3,4,512]{2,1,0:T(4,128)S(1)} %copy-done.1, f32[4,512]{1,0:T(4,128)S(1)} %copy-done.2, s32[1,512]{1,0:T(1,128)S(1)} %bitcast.22, s32[1,1024]{1,0:T(1,128)S(1)} %bitcast.19, ...), custom_call_target="tpu_custom_call" | custom-call | tf_op jit(solution)/shard_map/pallas_call | solution.py:228
  (1 shorter events, 0.0 us)
Async XLA Ops:
  0.6 0.7 %copy-start.1 = (f32[3,4,512]{2,1,0:T(4,128)S(1)}, f32[3,4,512]{2,1,0:T(4,128)}, u32[]{:S(2)}) copy-start(f32[3,4,512]{2,1,0:T(4,128)} %source_ref.5) | copy-start | bytes 73732
  0.6 0.8 %copy-start = (f32[16,1024]{1,0:T(8,128)S(1)}, f32[16,1024]{1,0:T(8,128)}, u32[]{:S(2)}) copy-start(f32[16,1024]{1,0:T(8,128)} %couple_ref.3) | copy-start | bytes 196612
  0.7 0.8 %copy-start.2 = (f32[4,512]{1,0:T(4,128)S(1)}, f32[4,512]{1,0:T(4,128)}, u32[]{:S(2)}) copy-start(f32[4,512]{1,0:T(4,128)} %relax_ref.5) | copy-start | bytes 24580
  0.7 0.8 %copy-start.5 = (s32[512]{0:T(512)S(1)}, s32[512]{0:T(512)}, u32[]{:S(2)}) copy-start(s32[512]{0:T(512)} %param.11) | copy-start | bytes 6148
  0.7 0.8 %copy-start.7 = (s32[1024]{0:T(1024)S(1)}, s32[1024]{0:T(1024)}, u32[]{:S(2)}) copy-start(s32[1024]{0:T(1024)} %param.13) | copy-start | bytes 12292
  0.7 0.8 %copy-start.3 = (s32[1024]{0:T(1024)S(1)}, s32[1024]{0:T(1024)}, u32[]{:S(2)}) copy-start(s32[1024]{0:T(1024)} %param.12) | copy-start | bytes 12292
  0.7 0.8 %copy-start.6 = (s32[1,128]{1,0:T(1,128)S(1)}, s32[1,128]{1,0:T(1,128)}, u32[]{:S(2)}) copy-start(s32[1,128]{1,0:T(1,128)} %fill_ref.5) | copy-start | bytes 1540
  26.3 7.2 %copy-start.4 = (f32[3,4,512]{2,1,0:T(4,128)S(1)}, f32[3,4,512]{2,1,0:T(4,128)}, u32[]{:S(2)}) copy-start(f32[3,4,512]{2,1,0:T(4,128)} %dev_ref.1) | copy-start | bytes 73732

commit v8 on v6

--- a/solution.py
+++ b/solution.py
@@ -105,7 +105,7 @@
 
 
 def first_chip(pools):
-    return pools * 13 // 16
+    return pools * 15 // 16
 
 
 def to_places(rows):

time: 61.9 us -> 62.7 us (1.013)
  blocking collectives: 56.9 us -> 57.7 us
    all_to_all x2, blocking collectives: 42.1 us -> 42.9 us  [exchange(): x = lax.all_to_all(x, 'pool', 0, 0, axis_index_groups=[members], tiled=True)]
where the time goes in v8:
time: 62.7 us; the launch traced here: 62.3 us
  blocking collectives  57.7 us (92%)
  Pallas kernels  3.08 us (5%)
  local copies, waits for them, and re-layouts  0.81 us (1%)
  between operations  0.72 us (1%)
    all_to_all x2, blocking collectives, exchange(): x = lax.all_to_all(x, 'pool', 0, 0, axis_index_groups=[members], tiled=True)  42.9 us
    all_to_all x2, blocking collectives, share(): lax.all_to_all(part, 'pb', 0, 0, axis_index_groups=[members], tiled=True)  14.8 us
    pallas_call x6, Pallas kernels, call(): pl.pallas_call(kernel, out_shape=out_shape, in_specs=[pl.BlockSpec(memory...  3.08 us

profile of v8, /device:TPU:1, one launch (start us, length us, event | category | flops | bytes accessed | tf_op | source)
XLA Modules:
  0.0 62.3 jit_solution(13170507206852757456)
XLA Ops:
  0.6 0.0 copy-start.1
  0.6 0.0 copy-start
  0.7 0.0 copy-start.2
  0.7 0.0 copy-start.5
  0.7 0.0 copy-start.7
  0.7 0.0 copy-start.3
  0.7 0.0 copy-start.6
  0.7 0.7 %copy-done.1 = f32[3,4,512]{2,1,0:T(4,128)S(1)} copy-done((f32[3,4,512]{2,1,0:T(4,128)S(1)}, f32[3,4,512]{2,1,0:T(4,128)}, u32[]{:S(2)}) %copy-start.1) | copy-done | bytes 24600
  1.4 0.1 copy-done
  1.5 0.0 copy-done.2
  1.5 0.0 copy-done.5
  1.5 0.0 copy-done.7
  1.5 0.0 copy-done.3
  1.5 0.0 copy-done.6
  1.5 0.6 shard_map.96
  2.1 24.6 %all_to_all.20 = f32[128,1,128]{2,1,0:T(1,128)S(1)} all-to-all(f32[128,1,128]{2,1,0:T(1,128)S(1)} %bitcast.16), channel_id=1, replica_groups={{484,480,488,492,496,500,504,508,0,4,8,12,16,20,24,28,32,36,40,44,48,52..., dimensions={0} | all-to-all | bytes 131072 | tf_op jit(solution)/shard_map/all_to_all | solution.py:240
  26.7 0.4 shard_map.97
  27.1 0.0 copy-start.4
  27.1 7.2 %all_to_all.21.parts_ref = f32[4,8,768]{2,1,0:T(8,128)S(1)} all-to-all(f32[4,8,768]{2,1,0:T(8,128)S(1)} %shard_map.97), channel_id=1, replica_groups={{2,3,0,1},{6,7,4,5},{10,11,8,9},{14,15,12,13},{18,19,16,17},{22,23,20,2..., dimensions={0} | all-to-all | bytes 196608 | tf_op jit(solution)/shard_map/all_to_all | solution.py:247
  34.3 0.0 copy-done.4
  34.3 0.6 %shard_map.98 = f32[256,128]{1,0:T(8,128)S(1)} custom-call(f32[4,8,768]{2,1,0:T(8,128)S(1)} %all_to_all.21.parts_ref, f32[128,128]{1,0:T(8,128)S(1)} %bitcast.11, f32[3,4,512]{2,1,0:T(4,128)S(1)} %copy-done.4, f32[3,4,512]{2,1,0:T(4,128)S(1)} %copy-done.1, f32[4,512]{1,0:T(4,128)S(1)} %copy-done.2, s32[1,512]{1,0:T(1,128)S(1)} %bitcast.21, ...), custom_call_target="tpu_custom_call" | custom-call | tf_op jit(solution)/shard_map/pallas_call | solution.py:225
  35.0 18.3 %all_to_all.22 = f32[128,2,128]{2,1,0:T(2,128)S(1)} all-to-all(f32[128,2,128]{2,1,0:T(2,128)S(1)} %bitcast.15), channel_id=1, replica_groups={{484,480,488,492,496,500,504,508,0,4,8,12,16,20,24,28,32,36,40,44,48,52..., dimensions={0} | all-to-all | bytes 262144 | tf_op jit(solution)/shard_map/all_to_all | solution.py:240
  53.3 0.4 shard_map.99
  53.7 7.6 %all_to_all.23.parts_ref = f32[4,8,768]{2,1,0:T(8,128)S(1)} all-to-all(f32[4,8,768]{2,1,0:T(8,128)S(1)} %shard_map.99), channel_id=1, replica_groups={{2,3,0,1},{6,7,4,5},{10,11,8,9},{14,15,12,13},{18,19,16,17},{22,23,20,2..., dimensions={0} | all-to-all | bytes 196608 | tf_op jit(solution)/shard_map/all_to_all | solution.py:247
  61.2 1.1 %shard_map.100 = (f32[3,4,512]{2,1,0:T(4,128)}, f32[16,1024]{1,0:T(8,128)}) custom-call(f32[4,8,768]{2,1,0:T(8,128)S(1)} %all_to_all.23.parts_ref, f32[256,128]{1,0:T(8,128)S(1)} %bitcast.14, f32[3,4,512]{2,1,0:T(4,128)S(1)} %copy-done.1, f32[4,512]{1,0:T(4,128)S(1)} %copy-done.2, s32[1,512]{1,0:T(1,128)S(1)} %bitcast.22, s32[1,1024]{1,0:T(1,128)S(1)} %bitcast.19, ...), custom_call_target="tpu_custom_call" | custom-call | tf_op jit(solution)/shard_map/pallas_call | solution.py:225
  (1 shorter events, 0.0 us)
Async XLA Ops:
  0.6 0.7 %copy-start.1 = (f32[3,4,512]{2,1,0:T(4,128)S(1)}, f32[3,4,512]{2,1,0:T(4,128)}, u32[]{:S(2)}) copy-start(f32[3,4,512]{2,1,0:T(4,128)} %source_ref.5) | copy-start | bytes 73732
  0.6 0.8 %copy-start = (f32[16,1024]{1,0:T(8,128)S(1)}, f32[16,1024]{1,0:T(8,128)}, u32[]{:S(2)}) copy-start(f32[16,1024]{1,0:T(8,128)} %couple_ref.3) | copy-start | bytes 196612
  0.7 0.8 %copy-start.2 = (f32[4,512]{1,0:T(4,128)S(1)}, f32[4,512]{1,0:T(4,128)}, u32[]{:S(2)}) copy-start(f32[4,512]{1,0:T(4,128)} %relax_ref.5) | copy-start | bytes 24580
  0.7 0.8 %copy-start.5 = (s32[512]{0:T(512)S(1)}, s32[512]{0:T(512)}, u32[]{:S(2)}) copy-start(s32[512]{0:T(512)} %param.11) | copy-start | bytes 6148
  0.7 0.8 %copy-start.7 = (s32[1024]{0:T(1024)S(1)}, s32[1024]{0:T(1024)}, u32[]{:S(2)}) copy-start(s32[1024]{0:T(1024)} %param.13) | copy-start | bytes 12292
  0.7 0.8 %copy-start.3 = (s32[1024]{0:T(1024)S(1)}, s32[1024]{0:T(1024)}, u32[]{:S(2)}) copy-start(s32[1024]{0:T(1024)} %param.12) | copy-start | bytes 12292
  0.7 0.8 %copy-start.6 = (s32[1,128]{1,0:T(1,128)S(1)}, s32[1,128]{1,0:T(1,128)}, u32[]{:S(2)}) copy-start(s32[1,128]{1,0:T(1,128)} %fill_ref.5) | copy-start | bytes 1540
  27.1 7.2 %copy-start.4 = (f32[3,4,512]{2,1,0:T(4,128)S(1)}, f32[3,4,512]{2,1,0:T(4,128)}, u32[]{:S(2)}) copy-start(f32[3,4,512]{2,1,0:T(4,128)} %dev_ref.1) | copy-start | bytes 73732

commit v9 on v8

--- a/solution.py
+++ b/solution.py
@@ -105,7 +105,7 @@
 
 
 def first_chip(pools):
-    return pools * 15 // 16
+    return pools * 9 // 16
 
 
 def to_places(rows):

time: 62.7 us -> 61.8 us (0.986)
  blocking collectives: 57.7 us -> 56.9 us
    all_to_all x2, blocking collectives: 42.9 us -> 42.1 us  [exchange(): x = lax.all_to_all(x, 'pool', 0, 0, axis_index_groups=[members], tiled=True)]
where the time goes in v9:
time: 61.8 us; the launch traced here: 61.5 us
  blocking collectives  56.9 us (92%)
  Pallas kernels  3.06 us (5%)
  local copies, waits for them, and re-layouts  0.81 us (1%)
  between operations  0.72 us (1%)
    all_to_all x2, blocking collectives, exchange(): x = lax.all_to_all(x, 'pool', 0, 0, axis_index_groups=[members], tiled=True)  42.1 us
    all_to_all x2, blocking collectives, share(): lax.all_to_all(part, 'pb', 0, 0, axis_index_groups=[members], tiled=True)  14.8 us
    pallas_call x6, Pallas kernels, call(): pl.pallas_call(kernel, out_shape=out_shape, in_specs=[pl.BlockSpec(memory...  3.06 us

profile of v9, /device:TPU:1, one launch (start us, length us, event | category | flops | bytes accessed | tf_op | source)
XLA Modules:
  0.0 61.5 jit_solution(16734119631733396185)
XLA Ops:
  0.6 0.0 copy-start.1
  0.6 0.0 copy-start
  0.7 0.0 copy-start.2
  0.7 0.0 copy-start.5
  0.7 0.0 copy-start.7
  0.7 0.0 copy-start.3
  0.7 0.0 copy-start.6
  0.7 0.7 %copy-done.1 = f32[3,4,512]{2,1,0:T(4,128)S(1)} copy-done((f32[3,4,512]{2,1,0:T(4,128)S(1)}, f32[3,4,512]{2,1,0:T(4,128)}, u32[]{:S(2)}) %copy-start.1) | copy-done | bytes 24600
  1.4 0.1 copy-done
  1.5 0.0 copy-done.2
  1.5 0.0 copy-done.5
  1.5 0.0 copy-done.7
  1.5 0.0 copy-done.3
  1.5 0.0 copy-done.6
  1.5 0.6 shard_map.96
  2.1 23.9 %all_to_all.20 = f32[128,1,128]{2,1,0:T(1,128)S(1)} all-to-all(f32[128,1,128]{2,1,0:T(1,128)S(1)} %bitcast.16), channel_id=1, replica_groups={{292,288,296,300,304,308,312,316,320,324,328,332,336,340,344,348,352,35..., dimensions={0} | all-to-all | bytes 131072 | tf_op jit(solution)/shard_map/all_to_all | solution.py:240
  26.0 0.4 shard_map.97
  26.3 0.0 copy-start.4
  26.3 7.2 %all_to_all.21.parts_ref = f32[4,8,768]{2,1,0:T(8,128)S(1)} all-to-all(f32[4,8,768]{2,1,0:T(8,128)S(1)} %shard_map.97), channel_id=1, replica_groups={{2,3,0,1},{6,7,4,5},{10,11,8,9},{14,15,12,13},{18,19,16,17},{22,23,20,2..., dimensions={0} | all-to-all | bytes 196608 | tf_op jit(solution)/shard_map/all_to_all | solution.py:247
  33.6 0.0 copy-done.4
  33.6 0.6 %shard_map.98 = f32[256,128]{1,0:T(8,128)S(1)} custom-call(f32[4,8,768]{2,1,0:T(8,128)S(1)} %all_to_all.21.parts_ref, f32[128,128]{1,0:T(8,128)S(1)} %bitcast.11, f32[3,4,512]{2,1,0:T(4,128)S(1)} %copy-done.4, f32[3,4,512]{2,1,0:T(4,128)S(1)} %copy-done.1, f32[4,512]{1,0:T(4,128)S(1)} %copy-done.2, s32[1,512]{1,0:T(1,128)S(1)} %bitcast.21, ...), custom_call_target="tpu_custom_call" | custom-call | tf_op jit(solution)/shard_map/pallas_call | solution.py:225
  34.2 18.2 %all_to_all.22 = f32[128,2,128]{2,1,0:T(2,128)S(1)} all-to-all(f32[128,2,128]{2,1,0:T(2,128)S(1)} %bitcast.15), channel_id=1, replica_groups={{292,288,296,300,304,308,312,316,320,324,328,332,336,340,344,348,352,35..., dimensions={0} | all-to-all | bytes 262144 | tf_op jit(solution)/shard_map/all_to_all | solution.py:240
  52.4 0.4 shard_map.99
  52.8 7.6 %all_to_all.23.parts_ref = f32[4,8,768]{2,1,0:T(8,128)S(1)} all-to-all(f32[4,8,768]{2,1,0:T(8,128)S(1)} %shard_map.99), channel_id=1, replica_groups={{2,3,0,1},{6,7,4,5},{10,11,8,9},{14,15,12,13},{18,19,16,17},{22,23,20,2..., dimensions={0} | all-to-all | bytes 196608 | tf_op jit(solution)/shard_map/all_to_all | solution.py:247
  60.4 1.1 %shard_map.100 = (f32[3,4,512]{2,1,0:T(4,128)}, f32[16,1024]{1,0:T(8,128)}) custom-call(f32[4,8,768]{2,1,0:T(8,128)S(1)} %all_to_all.23.parts_ref, f32[256,128]{1,0:T(8,128)S(1)} %bitcast.14, f32[3,4,512]{2,1,0:T(4,128)S(1)} %copy-done.1, f32[4,512]{1,0:T(4,128)S(1)} %copy-done.2, s32[1,512]{1,0:T(1,128)S(1)} %bitcast.22, s32[1,1024]{1,0:T(1,128)S(1)} %bitcast.19, ...), custom_call_target="tpu_custom_call" | custom-call | tf_op jit(solution)/shard_map/pallas_call | solution.py:225
  (1 shorter events, 0.0 us)
Async XLA Ops:
  0.6 0.7 %copy-start.1 = (f32[3,4,512]{2,1,0:T(4,128)S(1)}, f32[3,4,512]{2,1,0:T(4,128)}, u32[]{:S(2)}) copy-start(f32[3,4,512]{2,1,0:T(4,128)} %source_ref.5) | copy-start | bytes 73732
  0.6 0.8 %copy-start = (f32[16,1024]{1,0:T(8,128)S(1)}, f32[16,1024]{1,0:T(8,128)}, u32[]{:S(2)}) copy-start(f32[16,1024]{1,0:T(8,128)} %couple_ref.3) | copy-start | bytes 196612
  0.7 0.8 %copy-start.2 = (f32[4,512]{1,0:T(4,128)S(1)}, f32[4,512]{1,0:T(4,128)}, u32[]{:S(2)}) copy-start(f32[4,512]{1,0:T(4,128)} %relax_ref.5) | copy-start | bytes 24580
  0.7 0.8 %copy-start.5 = (s32[512]{0:T(512)S(1)}, s32[512]{0:T(512)}, u32[]{:S(2)}) copy-start(s32[512]{0:T(512)} %param.11) | copy-start | bytes 6148
  0.7 0.8 %copy-start.7 = (s32[1024]{0:T(1024)S(1)}, s32[1024]{0:T(1024)}, u32[]{:S(2)}) copy-start(s32[1024]{0:T(1024)} %param.13) | copy-start | bytes 12292
  0.7 0.8 %copy-start.3 = (s32[1024]{0:T(1024)S(1)}, s32[1024]{0:T(1024)}, u32[]{:S(2)}) copy-start(s32[1024]{0:T(1024)} %param.12) | copy-start | bytes 12292
  0.7 0.8 %copy-start.6 = (s32[1,128]{1,0:T(1,128)S(1)}, s32[1,128]{1,0:T(1,128)}, u32[]{:S(2)}) copy-start(s32[1,128]{1,0:T(1,128)} %fill_ref.5) | copy-start | bytes 1540
  26.3 7.2 %copy-start.4 = (f32[3,4,512]{2,1,0:T(4,128)S(1)}, f32[3,4,512]{2,1,0:T(4,128)}, u32[]{:S(2)}) copy-start(f32[3,4,512]{2,1,0:T(4,128)} %dev_ref.1) | copy-start | bytes 73732

commit v10 on v9

--- a/solution.py
+++ b/solution.py
@@ -105,7 +105,7 @@
 
 
 def first_chip(pools):
-    return pools * 9 // 16
+    return pools * 11 // 16
 
 
 def to_places(rows):
@@ -241,9 +241,9 @@
     return x.reshape(rows.shape)
 
 
-def share(part):
+def share(part, first):
     groups = lax.axis_size("pb")
-    members = [(place + groups // 2) % groups for place in range(groups)]
+    members = [(place + first) % groups for place in range(groups)]
     return lax.all_to_all(part, "pb", 0, 0, axis_index_groups=[members], tiled=True)
 
 
@@ -268,13 +268,13 @@
     )
     index = exchange(sent)
     gather = functools.partial(gather_kernel, states=states)
-    parts = share(call(gather, partial, [], index, index))
+    parts = share(call(gather, partial, [], index, index), 2)
     sent = call(
         second_kernel, sds((2 * pools, 128), F32), [flat],
         parts, index, deviation, adjoint_source, relax_time, window, src, bucket_fill, coupling,
     )
     rows = exchange(sent)
-    parts = share(call(gather, partial, [], rows, index))
+    parts = share(call(gather, partial, [], rows, index), 0)
     return call(
         last_kernel, (sds(adjoint_source.shape, F32), sds(coupling.shape, F32)), [flat],
         parts, rows, adjoint_source, relax_time, window, src, bucket_fill,

time: 61.8 us -> 63.3 us (1.024)
  blocking collectives: 56.9 us -> 58 us
    all_to_all x2, blocking collectives: 14.8 us -> 15.9 us  [share(): lax.all_to_all(part, 'pb', 0, 0, axis_index_groups=[members], tiled=True)]
where the time goes in v10:
time: 63.3 us; the launch traced here: 62.6 us
  blocking collectives  58 us (92%)
  Pallas kernels  3.07 us (5%)
  local copies, waits for them, and re-layouts  0.81 us (1%)
  between operations  0.72 us (1%)
    all_to_all x2, blocking collectives, exchange(): x = lax.all_to_all(x, 'pool', 0, 0, axis_index_groups=[members], tiled=True)  42.1 us
    all_to_all x2, blocking collectives, share(): lax.all_to_all(part, 'pb', 0, 0, axis_index_groups=[members], tiled=True)  15.9 us
    pallas_call x6, Pallas kernels, call(): pl.pallas_call(kernel, out_shape=out_shape, in_specs=[pl.BlockSpec(memory...  3.07 us

profile of v10, /device:TPU:1, one launch (start us, length us, event | category | flops | bytes accessed | tf_op | source)
XLA Modules:
  0.0 62.6 jit_solution(6059976812521695182)
XLA Ops:
  0.6 0.0 copy-start.1
  0.6 0.0 copy-start
  0.7 0.0 copy-start.2
  0.7 0.0 copy-start.5
  0.7 0.0 copy-start.7
  0.7 0.0 copy-start.3
  0.7 0.0 copy-start.6
  0.7 0.7 %copy-done.1 = f32[3,4,512]{2,1,0:T(4,128)S(1)} copy-done((f32[3,4,512]{2,1,0:T(4,128)S(1)}, f32[3,4,512]{2,1,0:T(4,128)}, u32[]{:S(2)}) %copy-start.1) | copy-done | bytes 24600
  1.4 0.1 copy-done
  1.5 0.0 copy-done.2
  1.5 0.0 copy-done.5
  1.5 0.0 copy-done.7
  1.5 0.0 copy-done.3
  1.5 0.0 copy-done.6
  1.5 0.6 shard_map.96
  2.1 23.8 %all_to_all.20 = f32[128,1,128]{2,1,0:T(1,128)S(1)} all-to-all(f32[128,1,128]{2,1,0:T(1,128)S(1)} %bitcast.16), channel_id=1, replica_groups={{356,352,360,364,368,372,376,380,384,388,392,396,400,404,408,412,416,42..., dimensions={0} | all-to-all | bytes 131072 | tf_op jit(solution)/shard_map/all_to_all | solution.py:240
  25.9 0.4 shard_map.97
  26.3 0.0 copy-start.4
  26.3 7.2 %all_to_all.21.parts_ref = f32[4,8,768]{2,1,0:T(8,128)S(1)} all-to-all(f32[4,8,768]{2,1,0:T(8,128)S(1)} %shard_map.97), channel_id=1, replica_groups={{2,3,0,1},{6,7,4,5},{10,11,8,9},{14,15,12,13},{18,19,16,17},{22,23,20,2..., dimensions={0} | all-to-all | bytes 196608 | tf_op jit(solution)/shard_map/all_to_all | solution.py:247
  33.5 0.0 copy-done.4
  33.5 0.6 %shard_map.98 = f32[256,128]{1,0:T(8,128)S(1)} custom-call(f32[4,8,768]{2,1,0:T(8,128)S(1)} %all_to_all.21.parts_ref, f32[128,128]{1,0:T(8,128)S(1)} %bitcast.11, f32[3,4,512]{2,1,0:T(4,128)S(1)} %copy-done.4, f32[3,4,512]{2,1,0:T(4,128)S(1)} %copy-done.1, f32[4,512]{1,0:T(4,128)S(1)} %copy-done.2, s32[1,512]{1,0:T(1,128)S(1)} %bitcast.21, ...), custom_call_target="tpu_custom_call" | custom-call | tf_op jit(solution)/shard_map/pallas_call | solution.py:225
  34.2 18.3 %all_to_all.22 = f32[128,2,128]{2,1,0:T(2,128)S(1)} all-to-all(f32[128,2,128]{2,1,0:T(2,128)S(1)} %bitcast.15), channel_id=1, replica_groups={{356,352,360,364,368,372,376,380,384,388,392,396,400,404,408,412,416,42..., dimensions={0} | all-to-all | bytes 262144 | tf_op jit(solution)/shard_map/all_to_all | solution.py:240
  52.5 0.4 shard_map.99
  52.8 8.7 %all_to_all.23.parts_ref = f32[4,8,768]{2,1,0:T(8,128)S(1)} all-to-all(f32[4,8,768]{2,1,0:T(8,128)S(1)} %shard_map.99), channel_id=1, replica_groups={{0,1,2,3},{4,5,6,7},{8,9,10,11},{12,13,14,15},{16,17,18,19},{20,21,22,2..., dimensions={0} | all-to-all | bytes 196608 | tf_op jit(solution)/shard_map/all_to_all | solution.py:247
  61.5 1.1 %shard_map.100 = (f32[3,4,512]{2,1,0:T(4,128)}, f32[16,1024]{1,0:T(8,128)}) custom-call(f32[4,8,768]{2,1,0:T(8,128)S(1)} %all_to_all.23.parts_ref, f32[256,128]{1,0:T(8,128)S(1)} %bitcast.14, f32[3,4,512]{2,1,0:T(4,128)S(1)} %copy-done.1, f32[4,512]{1,0:T(4,128)S(1)} %copy-done.2, s32[1,512]{1,0:T(1,128)S(1)} %bitcast.22, s32[1,1024]{1,0:T(1,128)S(1)} %bitcast.19, ...), custom_call_target="tpu_custom_call" | custom-call | tf_op jit(solution)/shard_map/pallas_call | solution.py:225
  (1 shorter events, 0.0 us)
Async XLA Ops:
  0.6 0.7 %copy-start.1 = (f32[3,4,512]{2,1,0:T(4,128)S(1)}, f32[3,4,512]{2,1,0:T(4,128)}, u32[]{:S(2)}) copy-start(f32[3,4,512]{2,1,0:T(4,128)} %source_ref.5) | copy-start | bytes 73732
  0.6 0.8 %copy-start = (f32[16,1024]{1,0:T(8,128)S(1)}, f32[16,1024]{1,0:T(8,128)}, u32[]{:S(2)}) copy-start(f32[16,1024]{1,0:T(8,128)} %couple_ref.3) | copy-start | bytes 196612
  0.7 0.8 %copy-start.2 = (f32[4,512]{1,0:T(4,128)S(1)}, f32[4,512]{1,0:T(4,128)}, u32[]{:S(2)}) copy-start(f32[4,512]{1,0:T(4,128)} %relax_ref.5) | copy-start | bytes 24580
  0.7 0.8 %copy-start.5 = (s32[512]{0:T(512)S(1)}, s32[512]{0:T(512)}, u32[]{:S(2)}) copy-start(s32[512]{0:T(512)} %param.11) | copy-start | bytes 6148
  0.7 0.8 %copy-start.7 = (s32[1024]{0:T(1024)S(1)}, s32[1024]{0:T(1024)}, u32[]{:S(2)}) copy-start(s32[1024]{0:T(1024)} %param.13) | copy-start | bytes 12292
  0.7 0.8 %copy-start.3 = (s32[1024]{0:T(1024)S(1)}, s32[1024]{0:T(1024)}, u32[]{:S(2)}) copy-start(s32[1024]{0:T(1024)} %param.12) | copy-start | bytes 12292
  0.7 0.8 %copy-start.6 = (s32[1,128]{1,0:T(1,128)S(1)}, s32[1,128]{1,0:T(1,128)}, u32[]{:S(2)}) copy-start(s32[1,128]{1,0:T(1,128)} %fill_ref.5) | copy-start | bytes 1540
  26.3 7.2 %copy-start.4 = (f32[3,4,512]{2,1,0:T(4,128)S(1)}, f32[3,4,512]{2,1,0:T(4,128)}, u32[]{:S(2)}) copy-start(f32[3,4,512]{2,1,0:T(4,128)} %dev_ref.1) | copy-start | bytes 73732

commit v11 on v6

--- a/solution.py
+++ b/solution.py
@@ -154,9 +154,10 @@
 
 
 def first_kernel(
-    zero_ref, couple_ref, source_ref, relax_ref, window_ref, src_ref, dst_ref, fill_ref, out_ref, flat_ref
+    zero_ref, couple_ref, source_ref, relax_ref, window_ref, src_ref, dst_ref, fill_ref, out_ref, live_ref, flat_ref
 ):
     live = live_row(fill_ref, src_ref.shape[1])
+    live_ref[...] = live
     relax = jnp.concatenate([relax_ref[...]] * 4, axis=0)
     moment = rows16(source_ref) * window16(window_ref) * relax
     terms = scatter_terms(pick(moment, src_ref[...]), live, couple_ref[...])
@@ -188,20 +189,19 @@
 
 
 def second_kernel(
-    parts_ref, index_ref, dev_ref, source_ref, relax_ref, window_ref, src_ref, fill_ref, couple_ref, out_ref, flat_ref
+    parts_ref, index_ref, dev_ref, source_ref, relax_ref, window_ref, src_ref, live_ref, couple_ref, out_ref, flat_ref
 ):
     senders = index_ref.shape[0]
     out_ref[pl.ds(1, senders, stride=2), :] = returned_rows(dev_ref, window_ref, index_ref)
     relax = jnp.concatenate([relax_ref[...]] * 4, axis=0)
     moment = relax * multiplier_of(parts_ref, source_ref, window_ref)
-    live = live_row(fill_ref, src_ref.shape[1])
-    terms = scatter_terms(select(moment, src_ref[...]), live, couple_ref[...])
+    terms = scatter_terms(select(moment, src_ref[...]), live_ref[...], couple_ref[...])
     rows = to_places(slots_to_rows(terms, flat_ref))
     out_ref[pl.ds(0, senders, stride=2), :] = rows
 
 
 def last_kernel(
-    parts_ref, rows_ref, source_ref, relax_ref, window_ref, src_ref, fill_ref, multiplier_ref, grad_ref, flat_ref
+    parts_ref, rows_ref, source_ref, relax_ref, window_ref, src_ref, live_ref, multiplier_ref, grad_ref, flat_ref
 ):
     owners = rows_ref.shape[0] // 2
     rows = from_places(rows_ref[pl.ds(1, owners, stride=2), :])
@@ -218,7 +218,7 @@
         far = fetched[4 * d : 4 * d + 4]
         term = repeat_rows(picked, 4 * d, 1, 4) * jnp.concatenate([far] * 4, axis=0)
         total = term if total is None else total + term
-    grad_ref[...] = total * live_row(fill_ref, src_ref.shape[1])
+    grad_ref[...] = total * live_ref[...]
 
 
 def call(kernel, out_shape, scratch, *operands, cost=None):
@@ -262,8 +262,8 @@
 
     cost = pl.CostEstimate(flops=10**10, bytes_accessed=0, transcendentals=0)
     zero = call(zero_kernel, sds((8, 128), F32), [], cost=cost)
-    sent = call(
-        first_kernel, sds((pools, 128), F32), [flat],
+    sent, live = call(
+        first_kernel, (sds((pools, 128), F32), sds((1, slots), F32)), [flat],
         zero, coupling, adjoint_source, relax_time, window, src, dst, bucket_fill,
     )
     index = exchange(sent)
@@ -271,13 +271,13 @@
     parts = share(call(gather, partial, [], index, index))
     sent = call(
         second_kernel, sds((2 * pools, 128), F32), [flat],
-        parts, index, deviation, adjoint_source, relax_time, window, src, bucket_fill, coupling,
+        parts, index, deviation, adjoint_source, relax_time, window, src, live, coupling,
     )
     rows = exchange(sent)
     parts = share(call(gather, partial, [], rows, index))
     return call(
         last_kernel, (sds(adjoint_source.shape, F32), sds(coupling.shape, F32)), [flat],
-        parts, rows, adjoint_source, relax_time, window, src, bucket_fill,
+        parts, rows, adjoint_source, relax_time, window, src, live,
     )
 
 

time: 61.9 us -> 61.8 us (level)
  no operation moved by 1% of the time
where the time goes in v11:
time: 61.8 us; the launch traced here: 61.5 us
  blocking collectives  56.9 us (92%)
  Pallas kernels  3.02 us (5%)
  local copies, waits for them, and re-layouts  0.81 us (1%)
  between operations  0.72 us (1%)
    all_to_all x2, blocking collectives, exchange(): x = lax.all_to_all(x, 'pool', 0, 0, axis_index_groups=[members], tiled=True)  42.1 us
    all_to_all x2, blocking collectives, share(): lax.all_to_all(part, 'pb', 0, 0, axis_index_groups=[members], tiled=True)  14.8 us
    pallas_call x6, Pallas kernels, call(): pl.pallas_call(kernel, out_shape=out_shape, in_specs=[pl.BlockSpec(memory...  3.02 us

profile of v11, /device:TPU:1, one launch (start us, length us, event | category | flops | bytes accessed | tf_op | source)
XLA Modules:
  0.0 61.5 jit_solution(2997866425397658183)
XLA Ops:
  0.6 0.0 copy-start.1
  0.6 0.0 copy-start
  0.7 0.0 copy-start.2
  0.7 0.0 copy-start.5
  0.7 0.0 copy-start.6
  0.7 0.0 copy-start.3
  0.7 0.0 copy-start.7
  0.7 0.7 %copy-done.1 = f32[3,4,512]{2,1,0:T(4,128)S(1)} copy-done((f32[3,4,512]{2,1,0:T(4,128)S(1)}, f32[3,4,512]{2,1,0:T(4,128)}, u32[]{:S(2)}) %copy-start.1) | copy-done | bytes 24600
  1.4 0.1 copy-done
  1.5 0.0 copy-done.2
  1.5 0.0 copy-done.5
  1.5 0.0 copy-done.6
  1.5 0.0 copy-done.3
  1.5 0.0 copy-done.7
  1.5 0.6 shard_map.96
  2.1 23.8 %all_to_all.20 = f32[128,1,128]{2,1,0:T(1,128)S(1)} all-to-all(f32[128,1,128]{2,1,0:T(1,128)S(1)} %bitcast.16), channel_id=1, replica_groups={{420,416,424,428,432,436,440,444,448,452,456,460,464,468,472,476,480,48..., dimensions={0} | all-to-all | bytes 131072 | tf_op jit(solution)/shard_map/all_to_all | solution.py:240
  25.9 0.4 shard_map.97
  26.3 0.0 copy-start.4
  26.3 7.2 %all_to_all.21.parts_ref = f32[4,8,768]{2,1,0:T(8,128)S(1)} all-to-all(f32[4,8,768]{2,1,0:T(8,128)S(1)} %shard_map.97), channel_id=1, replica_groups={{2,3,0,1},{6,7,4,5},{10,11,8,9},{14,15,12,13},{18,19,16,17},{22,23,20,2..., dimensions={0} | all-to-all | bytes 196608 | tf_op jit(solution)/shard_map/all_to_all | solution.py:247
  33.5 0.0 copy-done.4
  33.5 0.6 %shard_map.98 = f32[256,128]{1,0:T(8,128)S(1)} custom-call(f32[4,8,768]{2,1,0:T(8,128)S(1)} %all_to_all.21.parts_ref, f32[128,128]{1,0:T(8,128)S(1)} %bitcast.11, f32[3,4,512]{2,1,0:T(4,128)S(1)} %copy-done.4, f32[3,4,512]{2,1,0:T(4,128)S(1)} %copy-done.1, f32[4,512]{1,0:T(4,128)S(1)} %copy-done.2, s32[1,512]{1,0:T(1,128)S(1)} %bitcast.21, ...), custom_call_target="tpu_custom_call" | custom-call | tf_op jit(solution)/shard_map/pallas_call | solution.py:225
  34.2 18.3 %all_to_all.22 = f32[128,2,128]{2,1,0:T(2,128)S(1)} all-to-all(f32[128,2,128]{2,1,0:T(2,128)S(1)} %bitcast.15), channel_id=1, replica_groups={{420,416,424,428,432,436,440,444,448,452,456,460,464,468,472,476,480,48..., dimensions={0} | all-to-all | bytes 262144 | tf_op jit(solution)/shard_map/all_to_all | solution.py:240
  52.5 0.4 shard_map.99
  52.9 7.6 %all_to_all.23.parts_ref = f32[4,8,768]{2,1,0:T(8,128)S(1)} all-to-all(f32[4,8,768]{2,1,0:T(8,128)S(1)} %shard_map.99), channel_id=1, replica_groups={{2,3,0,1},{6,7,4,5},{10,11,8,9},{14,15,12,13},{18,19,16,17},{22,23,20,2..., dimensions={0} | all-to-all | bytes 196608 | tf_op jit(solution)/shard_map/all_to_all | solution.py:247
  60.4 1.0 %shard_map.100 = (f32[3,4,512]{2,1,0:T(4,128)}, f32[16,1024]{1,0:T(8,128)}) custom-call(f32[4,8,768]{2,1,0:T(8,128)S(1)} %all_to_all.23.parts_ref, f32[256,128]{1,0:T(8,128)S(1)} %bitcast.14, f32[3,4,512]{2,1,0:T(4,128)S(1)} %copy-done.1, f32[4,512]{1,0:T(4,128)S(1)} %copy-done.2, s32[1,512]{1,0:T(1,128)S(1)} %bitcast.22, s32[1,1024]{1,0:T(1,128)S(1)} %bitcast.19, ...), custom_call_target="tpu_custom_call" | custom-call | tf_op jit(solution)/shard_map/pallas_call | solution.py:225
  (1 shorter events, 0.0 us)
Async XLA Ops:
  0.6 0.7 %copy-start.1 = (f32[3,4,512]{2,1,0:T(4,128)S(1)}, f32[3,4,512]{2,1,0:T(4,128)}, u32[]{:S(2)}) copy-start(f32[3,4,512]{2,1,0:T(4,128)} %source_ref.5) | copy-start | bytes 73732
  0.6 0.8 %copy-start = (f32[16,1024]{1,0:T(8,128)S(1)}, f32[16,1024]{1,0:T(8,128)}, u32[]{:S(2)}) copy-start(f32[16,1024]{1,0:T(8,128)} %couple_ref.3) | copy-start | bytes 196612
  0.7 0.8 %copy-start.2 = (f32[4,512]{1,0:T(4,128)S(1)}, f32[4,512]{1,0:T(4,128)}, u32[]{:S(2)}) copy-start(f32[4,512]{1,0:T(4,128)} %relax_ref.5) | copy-start | bytes 24580
  0.7 0.8 %copy-start.5 = (s32[512]{0:T(512)S(1)}, s32[512]{0:T(512)}, u32[]{:S(2)}) copy-start(s32[512]{0:T(512)} %param.11) | copy-start | bytes 6148
  0.7 0.8 %copy-start.6 = (s32[1024]{0:T(1024)S(1)}, s32[1024]{0:T(1024)}, u32[]{:S(2)}) copy-start(s32[1024]{0:T(1024)} %param.13) | copy-start | bytes 12292
  0.7 0.8 %copy-start.3 = (s32[1024]{0:T(1024)S(1)}, s32[1024]{0:T(1024)}, u32[]{:S(2)}) copy-start(s32[1024]{0:T(1024)} %param.12) | copy-start | bytes 12292
  0.7 0.8 %copy-start.7 = (s32[1,128]{1,0:T(1,128)S(1)}, s32[1,128]{1,0:T(1,128)}, u32[]{:S(2)}) copy-start(s32[1,128]{1,0:T(1,128)} %fill_ref.1) | copy-start | bytes 1540
  26.3 7.2 %copy-start.4 = (f32[3,4,512]{2,1,0:T(4,128)S(1)}, f32[3,4,512]{2,1,0:T(4,128)}, u32[]{:S(2)}) copy-start(f32[3,4,512]{2,1,0:T(4,128)} %dev_ref.1) | copy-start | bytes 73732

commit v12 on v11

--- a/solution.py
+++ b/solution.py
@@ -105,7 +105,7 @@
 
 
 def first_chip(pools):
-    return pools * 13 // 16
+    return pools * 51 // 64
 
 
 def to_places(rows):

time: 61.8 us -> 63.8 us (1.032)
  blocking collectives: 56.9 us -> 58.9 us
    all_to_all x2, blocking collectives: 42.1 us -> 44.1 us  [exchange(): x = lax.all_to_all(x, 'pool', 0, 0, axis_index_groups=[members], tiled=True)]
where the time goes in v12:
time: 63.8 us; the launch traced here: 63.5 us
  blocking collectives  58.9 us (92%)
  Pallas kernels  3.01 us (5%)
  local copies, waits for them, and re-layouts  0.81 us (1%)
  between operations  0.73 us (1%)
    all_to_all x2, blocking collectives, exchange(): x = lax.all_to_all(x, 'pool', 0, 0, axis_index_groups=[members], tiled=True)  44.1 us
    all_to_all x2, blocking collectives, share(): lax.all_to_all(part, 'pb', 0, 0, axis_index_groups=[members], tiled=True)  14.8 us
    pallas_call x6, Pallas kernels, call(): pl.pallas_call(kernel, out_shape=out_shape, in_specs=[pl.BlockSpec(memory...  3.01 us

profile of v12, /device:TPU:1, one launch (start us, length us, event | category | flops | bytes accessed | tf_op | source)
XLA Modules:
  0.0 63.5 jit_solution(4090161434257063704)
XLA Ops:
  0.6 0.0 copy-start.1
  0.6 0.0 copy-start
  0.7 0.0 copy-start.2
  0.7 0.0 copy-start.5
  0.7 0.0 copy-start.6
  0.7 0.0 copy-start.3
  0.7 0.0 copy-start.7
  0.7 0.7 %copy-done.1 = f32[3,4,512]{2,1,0:T(4,128)S(1)} copy-done((f32[3,4,512]{2,1,0:T(4,128)S(1)}, f32[3,4,512]{2,1,0:T(4,128)}, u32[]{:S(2)}) %copy-start.1) | copy-done | bytes 24600
  1.4 0.1 copy-done
  1.5 0.0 copy-done.2
  1.5 0.0 copy-done.5
  1.5 0.0 copy-done.6
  1.5 0.0 copy-done.3
  1.5 0.0 copy-done.7
  1.5 0.6 shard_map.96
  2.1 25.8 %all_to_all.20 = f32[128,1,128]{2,1,0:T(1,128)S(1)} all-to-all(f32[128,1,128]{2,1,0:T(1,128)S(1)} %bitcast.16), channel_id=1, replica_groups={{412,408,416,420,424,428,432,436,440,444,448,452,456,460,464,468,472,47..., dimensions={0} | all-to-all | bytes 131072 | tf_op jit(solution)/shard_map/all_to_all | solution.py:240
  27.9 0.4 shard_map.97
  28.3 0.0 copy-start.4
  28.3 7.2 %all_to_all.21.parts_ref = f32[4,8,768]{2,1,0:T(8,128)S(1)} all-to-all(f32[4,8,768]{2,1,0:T(8,128)S(1)} %shard_map.97), channel_id=1, replica_groups={{2,3,0,1},{6,7,4,5},{10,11,8,9},{14,15,12,13},{18,19,16,17},{22,23,20,2..., dimensions={0} | all-to-all | bytes 196608 | tf_op jit(solution)/shard_map/all_to_all | solution.py:247
  35.5 0.0 copy-done.4
  35.5 0.7 %shard_map.98 = f32[256,128]{1,0:T(8,128)S(1)} custom-call(f32[4,8,768]{2,1,0:T(8,128)S(1)} %all_to_all.21.parts_ref, f32[128,128]{1,0:T(8,128)S(1)} %bitcast.11, f32[3,4,512]{2,1,0:T(4,128)S(1)} %copy-done.4, f32[3,4,512]{2,1,0:T(4,128)S(1)} %copy-done.1, f32[4,512]{1,0:T(4,128)S(1)} %copy-done.2, s32[1,512]{1,0:T(1,128)S(1)} %bitcast.21, ...), custom_call_target="tpu_custom_call" | custom-call | tf_op jit(solution)/shard_map/pallas_call | solution.py:225
  36.2 18.3 %all_to_all.22 = f32[128,2,128]{2,1,0:T(2,128)S(1)} all-to-all(f32[128,2,128]{2,1,0:T(2,128)S(1)} %bitcast.15), channel_id=1, replica_groups={{412,408,416,420,424,428,432,436,440,444,448,452,456,460,464,468,472,47..., dimensions={0} | all-to-all | bytes 262144 | tf_op jit(solution)/shard_map/all_to_all | solution.py:240
  54.5 0.4 shard_map.99
  54.9 7.6 %all_to_all.23.parts_ref = f32[4,8,768]{2,1,0:T(8,128)S(1)} all-to-all(f32[4,8,768]{2,1,0:T(8,128)S(1)} %shard_map.99), channel_id=1, replica_groups={{2,3,0,1},{6,7,4,5},{10,11,8,9},{14,15,12,13},{18,19,16,17},{22,23,20,2..., dimensions={0} | all-to-all | bytes 196608 | tf_op jit(solution)/shard_map/all_to_all | solution.py:247
  62.4 1.0 %shard_map.100 = (f32[3,4,512]{2,1,0:T(4,128)}, f32[16,1024]{1,0:T(8,128)}) custom-call(f32[4,8,768]{2,1,0:T(8,128)S(1)} %all_to_all.23.parts_ref, f32[256,128]{1,0:T(8,128)S(1)} %bitcast.14, f32[3,4,512]{2,1,0:T(4,128)S(1)} %copy-done.1, f32[4,512]{1,0:T(4,128)S(1)} %copy-done.2, s32[1,512]{1,0:T(1,128)S(1)} %bitcast.22, s32[1,1024]{1,0:T(1,128)S(1)} %bitcast.19, ...), custom_call_target="tpu_custom_call" | custom-call | tf_op jit(solution)/shard_map/pallas_call | solution.py:225
  (1 shorter events, 0.0 us)
Async XLA Ops:
  0.6 0.7 %copy-start.1 = (f32[3,4,512]{2,1,0:T(4,128)S(1)}, f32[3,4,512]{2,1,0:T(4,128)}, u32[]{:S(2)}) copy-start(f32[3,4,512]{2,1,0:T(4,128)} %source_ref.5) | copy-start | bytes 73732
  0.6 0.8 %copy-start = (f32[16,1024]{1,0:T(8,128)S(1)}, f32[16,1024]{1,0:T(8,128)}, u32[]{:S(2)}) copy-start(f32[16,1024]{1,0:T(8,128)} %couple_ref.3) | copy-start | bytes 196612
  0.7 0.8 %copy-start.2 = (f32[4,512]{1,0:T(4,128)S(1)}, f32[4,512]{1,0:T(4,128)}, u32[]{:S(2)}) copy-start(f32[4,512]{1,0:T(4,128)} %relax_ref.5) | copy-start | bytes 24580
  0.7 0.8 %copy-start.5 = (s32[512]{0:T(512)S(1)}, s32[512]{0:T(512)}, u32[]{:S(2)}) copy-start(s32[512]{0:T(512)} %param.11) | copy-start | bytes 6148
  0.7 0.8 %copy-start.6 = (s32[1024]{0:T(1024)S(1)}, s32[1024]{0:T(1024)}, u32[]{:S(2)}) copy-start(s32[1024]{0:T(1024)} %param.13) | copy-start | bytes 12292
  0.7 0.8 %copy-start.3 = (s32[1024]{0:T(1024)S(1)}, s32[1024]{0:T(1024)}, u32[]{:S(2)}) copy-start(s32[1024]{0:T(1024)} %param.12) | copy-start | bytes 12292
  0.7 0.8 %copy-start.7 = (s32[1,128]{1,0:T(1,128)S(1)}, s32[1,128]{1,0:T(1,128)}, u32[]{:S(2)}) copy-start(s32[1,128]{1,0:T(1,128)} %fill_ref.1) | copy-start | bytes 1540
  28.3 7.2 %copy-start.4 = (f32[3,4,512]{2,1,0:T(4,128)S(1)}, f32[3,4,512]{2,1,0:T(4,128)}, u32[]{:S(2)}) copy-start(f32[3,4,512]{2,1,0:T(4,128)} %dev_ref.1) | copy-start | bytes 73732

commit v13 on v12

--- a/solution.py
+++ b/solution.py
@@ -105,7 +105,7 @@
 
 
 def first_chip(pools):
-    return pools * 51 // 64
+    return pools * 53 // 64
 
 
 def to_places(rows):

time: 63.8 us -> 62 us (0.972)
  blocking collectives: 58.9 us -> 57.1 us
    all_to_all x2, blocking collectives: 44.1 us -> 42.3 us  [exchange(): x = lax.all_to_all(x, 'pool', 0, 0, axis_index_groups=[members], tiled=True)]
where the time goes in v13:
time: 62 us; the launch traced here: 61.6 us
  blocking collectives  57.1 us (92%)
  Pallas kernels  3.02 us (5%)
  local copies, waits for them, and re-layouts  0.81 us (1%)
  between operations  0.72 us (1%)
    all_to_all x2, blocking collectives, exchange(): x = lax.all_to_all(x, 'pool', 0, 0, axis_index_groups=[members], tiled=True)  42.3 us
    all_to_all x2, blocking collectives, share(): lax.all_to_all(part, 'pb', 0, 0, axis_index_groups=[members], tiled=True)  14.8 us
    pallas_call x6, Pallas kernels, call(): pl.pallas_call(kernel, out_shape=out_shape, in_specs=[pl.BlockSpec(memory...  3.02 us

profile of v13, /device:TPU:1, one launch (start us, length us, event | category | flops | bytes accessed | tf_op | source)
XLA Modules:
  0.0 61.6 jit_solution(4802508273431968324)
XLA Ops:
  0.6 0.0 copy-start.1
  0.6 0.0 copy-start
  0.7 0.0 copy-start.2
  0.7 0.0 copy-start.5
  0.7 0.0 copy-start.6
  0.7 0.0 copy-start.3
  0.7 0.0 copy-start.7
  0.7 0.7 %copy-done.1 = f32[3,4,512]{2,1,0:T(4,128)S(1)} copy-done((f32[3,4,512]{2,1,0:T(4,128)S(1)}, f32[3,4,512]{2,1,0:T(4,128)}, u32[]{:S(2)}) %copy-start.1) | copy-done | bytes 24600
  1.4 0.1 copy-done
  1.5 0.0 copy-done.2
  1.5 0.0 copy-done.5
  1.5 0.0 copy-done.6
  1.5 0.0 copy-done.3
  1.5 0.0 copy-done.7
  1.5 0.6 shard_map.96
  2.1 24.0 %all_to_all.20 = f32[128,1,128]{2,1,0:T(1,128)S(1)} all-to-all(f32[128,1,128]{2,1,0:T(1,128)S(1)} %bitcast.16), channel_id=1, replica_groups={{428,424,432,436,440,444,448,452,456,460,464,468,472,476,480,484,488,49..., dimensions={0} | all-to-all | bytes 131072 | tf_op jit(solution)/shard_map/all_to_all | solution.py:240
  26.1 0.4 shard_map.97
  26.5 0.0 copy-start.4
  26.5 7.2 %all_to_all.21.parts_ref = f32[4,8,768]{2,1,0:T(8,128)S(1)} all-to-all(f32[4,8,768]{2,1,0:T(8,128)S(1)} %shard_map.97), channel_id=1, replica_groups={{2,3,0,1},{6,7,4,5},{10,11,8,9},{14,15,12,13},{18,19,16,17},{22,23,20,2..., dimensions={0} | all-to-all | bytes 196608 | tf_op jit(solution)/shard_map/all_to_all | solution.py:247
  33.7 0.0 copy-done.4
  33.7 0.6 %shard_map.98 = f32[256,128]{1,0:T(8,128)S(1)} custom-call(f32[4,8,768]{2,1,0:T(8,128)S(1)} %all_to_all.21.parts_ref, f32[128,128]{1,0:T(8,128)S(1)} %bitcast.11, f32[3,4,512]{2,1,0:T(4,128)S(1)} %copy-done.4, f32[3,4,512]{2,1,0:T(4,128)S(1)} %copy-done.1, f32[4,512]{1,0:T(4,128)S(1)} %copy-done.2, s32[1,512]{1,0:T(1,128)S(1)} %bitcast.21, ...), custom_call_target="tpu_custom_call" | custom-call | tf_op jit(solution)/shard_map/pallas_call | solution.py:225
  34.4 18.2 %all_to_all.22 = f32[128,2,128]{2,1,0:T(2,128)S(1)} all-to-all(f32[128,2,128]{2,1,0:T(2,128)S(1)} %bitcast.15), channel_id=1, replica_groups={{428,424,432,436,440,444,448,452,456,460,464,468,472,476,480,484,488,49..., dimensions={0} | all-to-all | bytes 262144 | tf_op jit(solution)/shard_map/all_to_all | solution.py:240
  52.6 0.4 shard_map.99
  53.0 7.6 %all_to_all.23.parts_ref = f32[4,8,768]{2,1,0:T(8,128)S(1)} all-to-all(f32[4,8,768]{2,1,0:T(8,128)S(1)} %shard_map.99), channel_id=1, replica_groups={{2,3,0,1},{6,7,4,5},{10,11,8,9},{14,15,12,13},{18,19,16,17},{22,23,20,2..., dimensions={0} | all-to-all | bytes 196608 | tf_op jit(solution)/shard_map/all_to_all | solution.py:247
  60.6 1.0 %shard_map.100 = (f32[3,4,512]{2,1,0:T(4,128)}, f32[16,1024]{1,0:T(8,128)}) custom-call(f32[4,8,768]{2,1,0:T(8,128)S(1)} %all_to_all.23.parts_ref, f32[256,128]{1,0:T(8,128)S(1)} %bitcast.14, f32[3,4,512]{2,1,0:T(4,128)S(1)} %copy-done.1, f32[4,512]{1,0:T(4,128)S(1)} %copy-done.2, s32[1,512]{1,0:T(1,128)S(1)} %bitcast.22, s32[1,1024]{1,0:T(1,128)S(1)} %bitcast.19, ...), custom_call_target="tpu_custom_call" | custom-call | tf_op jit(solution)/shard_map/pallas_call | solution.py:225
  (1 shorter events, 0.0 us)
Async XLA Ops:
  0.6 0.7 %copy-start.1 = (f32[3,4,512]{2,1,0:T(4,128)S(1)}, f32[3,4,512]{2,1,0:T(4,128)}, u32[]{:S(2)}) copy-start(f32[3,4,512]{2,1,0:T(4,128)} %source_ref.5) | copy-start | bytes 73732
  0.6 0.8 %copy-start = (f32[16,1024]{1,0:T(8,128)S(1)}, f32[16,1024]{1,0:T(8,128)}, u32[]{:S(2)}) copy-start(f32[16,1024]{1,0:T(8,128)} %couple_ref.3) | copy-start | bytes 196612
  0.7 0.8 %copy-start.2 = (f32[4,512]{1,0:T(4,128)S(1)}, f32[4,512]{1,0:T(4,128)}, u32[]{:S(2)}) copy-start(f32[4,512]{1,0:T(4,128)} %relax_ref.5) | copy-start | bytes 24580
  0.7 0.8 %copy-start.5 = (s32[512]{0:T(512)S(1)}, s32[512]{0:T(512)}, u32[]{:S(2)}) copy-start(s32[512]{0:T(512)} %param.11) | copy-start | bytes 6148
  0.7 0.8 %copy-start.6 = (s32[1024]{0:T(1024)S(1)}, s32[1024]{0:T(1024)}, u32[]{:S(2)}) copy-start(s32[1024]{0:T(1024)} %param.13) | copy-start | bytes 12292
  0.7 0.8 %copy-start.3 = (s32[1024]{0:T(1024)S(1)}, s32[1024]{0:T(1024)}, u32[]{:S(2)}) copy-start(s32[1024]{0:T(1024)} %param.12) | copy-start | bytes 12292
  0.7 0.8 %copy-start.7 = (s32[1,128]{1,0:T(1,128)S(1)}, s32[1,128]{1,0:T(1,128)}, u32[]{:S(2)}) copy-start(s32[1,128]{1,0:T(1,128)} %fill_ref.1) | copy-start | bytes 1540
  26.5 7.2 %copy-start.4 = (f32[3,4,512]{2,1,0:T(4,128)S(1)}, f32[3,4,512]{2,1,0:T(4,128)}, u32[]{:S(2)}) copy-start(f32[3,4,512]{2,1,0:T(4,128)} %dev_ref.1) | copy-start | bytes 73732
